TPU v7x, 128 devices: a whole 4x4x4 slice. The times are simulated.
128 devices in a mesh: ep: 32 (over z, y_lo, x), rep: 4 (over y_hi, core).
Axes of the slice: x: 4, y: 4 (y_hi: 2, y_lo: 2; y = y_hi * 2 + y_lo), z: 4, core: 2. Of those that a mesh axis runs over, the one named last changes fastest.
Arguments:
- tokens: bfloat16 [16384, 4096], P(('ep', 'rep')), may hold values from -6 to 6
- expert_ids: int32 [16384, 2], P(('ep', 'rep')), may hold values from 0 to 63, as said below
- route_weights: float32 [16384, 2], P(('ep', 'rep')), may hold values from 0.1 to 1
- w_gate: bfloat16 [4, 4096, 8192], P('rep', None, 'ep'), may hold values from -0.09375 to 0.09375
- w_up: bfloat16 [4, 4096, 8192], P('rep', None, 'ep'), may hold values from -0.09375 to 0.09375
- w_down: bfloat16 [4, 8192, 4096], P('rep', 'ep'), may hold values from -0.0625 to 0.0625
- cotangent: bfloat16 [16384, 4096], P(('ep', 'rep')), may hold values from -6 to 6
Outputs:
- mixed: bfloat16 [16384, 4096], P(('ep', 'rep'))
- grad_tokens: bfloat16 [16384, 4096], P(('ep', 'rep'))
- grad_gate: bfloat16 [4, 4096, 8192], P('rep', None, 'ep')
- grad_up: bfloat16 [4, 4096, 8192], P('rep', None, 'ep')
- grad_down: bfloat16 [4, 8192, 4096], P('rep', 'ep')
Inputs may be any that keep to these rules, and one draw needn't show every extreme that they name: `expert_ids`: A token's two experts differ. Among the rows of one device, each expert below 4 is named at most 4 times; one of them is named exactly 4 times by every device.
All inputs are finite; a program needn't handle non-finite values.
Results may differ from a plain program's by a relative error of at most 0.0058.
Values may be sent and summed in bfloat16 or wider, within the bound.
A program may use at most 128 MiB of HBM per device.

v0:
```python
import jax
import jax.numpy as jnp
from jax import lax
from jax.sharding import PartitionSpec as P

CAP = 4


def deliver(buffer):
    n_rep = lax.axis_size("rep")
    width = buffer.shape[1]
    traded = lax.all_to_all(
        buffer.reshape(n_rep, CAP, width), "rep", split_axis=0, concat_axis=0, tiled=True
    )
    own_rows = traded.reshape(n_rep * CAP, width)
    gathered = lax.all_gather(own_rows, "ep", axis=0, tiled=True)
    return (gathered, own_rows)


def give_back(results):
    n_rep = lax.axis_size("rep")
    return lax.all_to_all(
        results.reshape(n_rep, CAP, results.shape[1]),
        "rep",
        split_axis=0,
        concat_axis=0,
        tiled=True,
    )


def local(tokens, expert_ids, route_weights, w_gate, w_up, w_down, cotangent):
    n_rep = lax.axis_size("rep")
    tok_dev = tokens.shape[0]
    width = tokens.shape[1]
    routes = 2 * tok_dev
    block_rows = n_rep * CAP
    flat_e = expert_ids.reshape(-1)
    inside = flat_e < n_rep
    onehot = (flat_e[:, None] == jnp.arange(n_rep, dtype=jnp.int32)[None, :]).astype(jnp.int32)
    before = jnp.cumsum(onehot, axis=0) - onehot
    position = jnp.sum(before * onehot, axis=1)
    slot = jnp.where(inside, flat_e * CAP + position, block_rows)
    token_of = jnp.arange(routes, dtype=jnp.int32) // 2

    def pack(values):
        return jnp.zeros((block_rows + 1, width), jnp.bfloat16).at[slot].set(values)[:block_rows]

    def unpack(returned):
        padded = jnp.concatenate(
            [returned.reshape(block_rows, width), jnp.zeros((1, width), jnp.bfloat16)], axis=0
        )
        return padded[slot].astype(jnp.float32).reshape(tok_dev, 2, width)

    gathered, own_rows = deliver(pack(tokens[token_of]))
    pre_gate = jnp.dot(gathered, w_gate[0], preferred_element_type=jnp.float32)
    pre_up = jnp.dot(gathered, w_up[0], preferred_element_type=jnp.float32)
    logistic = jax.nn.sigmoid(pre_gate)
    activated = pre_gate * logistic
    hidden = (activated * pre_up).astype(jnp.bfloat16)
    routed = lax.psum_scatter(
        jnp.dot(hidden, w_down[0], preferred_element_type=jnp.float32),
        "ep",
        scatter_dimension=0,
        tiled=True,
    ).astype(jnp.bfloat16)
    arrived = unpack(give_back(routed))
    mixed = (
        route_weights[:, 0, None] * arrived[:, 0] + route_weights[:, 1, None] * arrived[:, 1]
    ).astype(jnp.bfloat16)
    upstream = (
        (route_weights[:, :, None] * cotangent[:, None, :].astype(jnp.float32))
        .astype(jnp.bfloat16)
        .reshape(routes, width)
    )
    upstream_rows, ignored = deliver(pack(upstream))
    d_act = jnp.einsum("rd,fd->rf", upstream_rows, w_down[0], preferred_element_type=jnp.float32)
    d_up = (d_act * activated).astype(jnp.bfloat16)
    d_gate = (d_act * pre_up * logistic * (1.0 + pre_gate * (1.0 - logistic))).astype(jnp.bfloat16)
    first = jnp.einsum("rf,df->rd", d_gate, w_gate[0], preferred_element_type=jnp.float32)
    row_grads = lax.psum_scatter(
        first + jnp.einsum("rf,df->rd", d_up, w_up[0], preferred_element_type=jnp.float32),
        "ep",
        scatter_dimension=0,
        tiled=True,
    ).astype(jnp.bfloat16)
    collected = unpack(give_back(row_grads))
    grad_tokens = (collected[:, 0] + collected[:, 1]).astype(jnp.bfloat16)
    row_source = lax.all_gather(own_rows, "ep", axis=0, tiled=True)
    grad_gate = jnp.einsum(
        "rd,rf->df", row_source, d_gate, preferred_element_type=jnp.float32
    ).astype(jnp.bfloat16)[None]
    grad_up = jnp.einsum("rd,rf->df", row_source, d_up, preferred_element_type=jnp.float32).astype(
        jnp.bfloat16
    )[None]
    grad_down = jnp.einsum(
        "rf,rd->fd", hidden, upstream_rows, preferred_element_type=jnp.float32
    ).astype(jnp.bfloat16)[None]
    return (mixed, grad_tokens, grad_gate, grad_up, grad_down)


def solution(mesh):
    placed = (
        P(("ep", "rep"), None),
        P(("ep", "rep"), None),
        P(("ep", "rep"), None),
        P("rep", None, "ep"),
        P("rep", None, "ep"),
        P("rep", "ep", None),
        P(("ep", "rep"), None),
    )
    return jax.shard_map(
        local,
        mesh=mesh,
        in_specs=placed,
        out_specs=(
            P(("ep", "rep"), None),
            P(("ep", "rep"), None),
            P("rep", None, "ep"),
            P("rep", None, "ep"),
            P("rep", "ep", None),
        ),
        check_vma=False,
    )
```

profile of v0, /device:TPU:1, one launch (start us, length us, event | category | flops | bytes accessed | tf_op | source)
XLA Modules:
  0.0 772.3 jit_solution(4353141673496977024)
XLA Ops:
  12.1 8.5 %scatter_custom_fusion = bf16[17,4096]{1,0:T(8,128)(2,1)S(1)} fusion(s32[256]{0:T(256)S(1)} %bitcast.80, bf16[128,4096]{1,0:T(8,128)(2,1)} %param.7, s32[1024]{0:T(1024)S(1)} %pad_clamp_fusion.1, bf16[]{:T(256)} %constant.26.clone.1), kind=kCustom, calls=%fused_computation.33 | custom fusion | bytes 139776 | tf_op jit(solution)/shard_map/scatter | solution.py:46
  20.7 10.9 %all_to_all.20 = bf16[4,4,4096]{2,1,0:T(4,128)(2,1)S(1)} all-to-all(bf16[4,4,4096]{2,1,0:T(4,128)(2,1)S(1)} %reshape.155), channel_id=1, replica_groups=mesh['ep'=32,'rep'=4] {'rep'}, dimensions={0} | all-to-all | bytes 262144 | tf_op jit(solution)/shard_map/all_to_all | solution.py:12
  33.4 4.1 mul.88
  37.5 6.1 mul.89
  43.6 5.0 scatter_custom_fusion.1
  48.7 9.9 %all_to_all.21 = bf16[4,4,4096]{2,1,0:T(4,128)(2,1)S(1)} all-to-all(bf16[4,4,4096]{2,1,0:T(4,128)(2,1)S(1)} %reshape.159), channel_id=1, replica_groups=mesh['ep'=32,'rep'=4] {'rep'}, dimensions={0} | all-to-all | bytes 262144 | tf_op jit(solution)/shard_map/all_to_all | solution.py:12
  59.4 111.3 %all-gather.3.cloned.1.call-done = bf16[512,4096]{1,0:T(8,128)(2,1)} async-done(((bf16[16,4096]{1,0:T(8,128)(2,1)}), bf16[512,4096]{1,0:T(8,128)(2,1)}) %all-gather.3.cloned.1.call-update) | async-done | bytes 4194320 | tf_op jit(solution)/shard_map/all_gather | solution.py:16
  170.7 4.2 fusion.14
  177.4 151.7 %all-gather.5.cloned.1.call-done = bf16[512,4096]{1,0:T(8,128)(2,1)} async-done(((bf16[16,4096]{1,0:T(8,128)(2,1)}), bf16[512,4096]{1,0:T(8,128)(2,1)}) %all-gather.5.cloned.1.call-update) | async-done | bytes 4194320 | tf_op jit(solution)/shard_map/all_gather | solution.py:16
  329.1 3.8 multiply_convert_fusion.2
  334.6 4.7 convolution_add_fusion
  339.7 4.5 fusion.11
  344.9 5.0 fusion.1
  352.5 163.4 %reduce-scatter.5.cloned.1.call-done = f32[16,4096]{1,0:T(8,128)} async-done(((f32[512,4096]{1,0:T(8,128)}), f32[16,4096]{1,0:T(8,128)}) %reduce-scatter.5.cloned.1.call-update) | async-done | bytes 262160 | tf_op jit(solution)/shard_map/reduce_scatter | solution.py:80
  517.6 26.7 %all-to-all-start.3 = ((bf16[4,4,4096]{2,1,0:T(4,128)(2,1)}), bf16[4,4,4096]{2,1,0:T(4,128)(2,1)S(1)}, u32[]{:S(2)}, u32[]{:S(2)}) async-start(bf16[4,4,4096]{2,1,0:T(4,128)(2,1)} %reshape.161), calls=%async_computation.5 | async-start | bytes 262144 | tf_op jit(solution)/shard_map/all_to_all | solution.py:22
  544.2 5.0 fusion.2
  549.2 143.5 %reduce-scatter.3.cloned.1.call-done = f32[16,4096]{1,0:T(8,128)} async-done(((f32[512,4096]{1,0:T(8,128)}), f32[16,4096]{1,0:T(8,128)}) %reduce-scatter.3.cloned.1.call-update) | async-done | bytes 262160 | tf_op jit(solution)/shard_map/reduce_scatter | solution.py:60
  694.4 27.5 %all-to-all-start.1 = ((bf16[4,4,4096]{2,1,0:T(4,128)(2,1)}), bf16[4,4,4096]{2,1,0:T(4,128)(2,1)S(1)}, u32[]{:S(2)}, u32[]{:S(2)}) async-start(bf16[4,4,4096]{2,1,0:T(4,128)(2,1)} %reshape.157), calls=%async_computation.2 | async-start | bytes 262144 | tf_op jit(solution)/shard_map/all_to_all | solution.py:22
  725.1 5.5 reshape.164
  730.5 9.9 %fusion.30 = (f32[128,1,4096]{2,1,0:T(1,128)}, f32[128,1,4096]{2,1,0:T(1,128)}) fusion(f32[128,2,4096]{2,1,0:T(2,128)} %reshape.164), kind=kLoop, calls=%fused_computation.63 | loop fusion | bytes 8388608 | tf_op jit(solution)/shard_map/slice | solution.py:87
  740.4 3.2 gather_fusion
  743.7 5.6 reshape.163
  749.3 8.0 %fusion.31 = (f32[128,1,4096]{2,1,0:T(1,128)S(1)}, f32[128,1,4096]{2,1,0:T(1,128)S(1)}) fusion(f32[128,2,4096]{2,1,0:T(2,128)} %reshape.163), kind=kLoop, calls=%fused_computation.64 | loop fusion | bytes 8388608 | tf_op jit(solution)/shard_map/slice | solution.py:68
  760.6 5.0 fusion.7
  (76 shorter events, 25.3 us)
Async XLA Ops:
  7.2 322.0 %copy-start = (bf16[1,256,4096]{2,1,0:T(8,128)(2,1)S(1)}, bf16[1,256,4096]{2,1,0:T(8,128)(2,1)}, u32[]{:S(2)}) copy-start(bf16[1,256,4096]{2,1,0:T(8,128)(2,1)} %param.12) | copy-start | bytes 6291460
  7.2 26.3 %copy-start.7 = (bf16[128,4096]{1,0:T(8,128)(2,1)S(1)}, bf16[128,4096]{1,0:T(8,128)(2,1)}, u32[]{:S(2)}) copy-start(bf16[128,4096]{1,0:T(8,128)(2,1)} %param.13) | copy-start | bytes 3145732
  7.2 163.5 %all-gather.3.cloned.1.call-start = ((), (), s32[]{:S(2)}) async-start(), calls=%async_computation.6 | async-start | bytes 4325376 | tf_op jit(solution)/shard_map/all_gather | solution.py:16
  32.3 296.9 %all-gather.5.cloned.1.call-start = ((), (), s32[]{:S(2)}) async-start(), calls=%async_computation.8 | async-start | bytes 4325376 | tf_op jit(solution)/shard_map/all_gather | solution.py:16
  59.3 456.6 %reduce-scatter.5.cloned.1.call-start = ((), (), s32[]{:S(2)}) async-start(), calls=%async_computation.9 | async-start | bytes 8650752 | tf_op jit(solution)/shard_map/reduce_scatter | solution.py:80
  170.7 4.3 copy-start.4
  170.7 4.7 copy-start.9
  329.1 3.9 copy-start.5
  333.0 1.6 copy-start.6
  339.3 353.4 %reduce-scatter.3.cloned.1.call-start = ((), (), s32[]{:S(2)}) async-start(), calls=%async_computation.7 | async-start | bytes 8650752 | tf_op jit(solution)/shard_map/reduce_scatter | solution.py:60
  344.2 0.7 copy-start.8
  344.9 5.0 copy-start.10
  517.6 176.8 %all-to-all-start.3 = ((bf16[4,4,4096]{2,1,0:T(4,128)(2,1)}), bf16[4,4,4096]{2,1,0:T(4,128)(2,1)S(1)}, u32[]{:S(2)}, u32[]{:S(2)}) async-start(bf16[4,4,4096]{2,1,0:T(4,128)(2,1)} %reshape.161), calls=%async_computation.5 | async-start | bytes 262144 | tf_op jit(solution)/shard_map/all_to_all | solution.py:22
  694.4 46.0 %all-to-all-start.1 = ((bf16[4,4,4096]{2,1,0:T(4,128)(2,1)}), bf16[4,4,4096]{2,1,0:T(4,128)(2,1)S(1)}, u32[]{:S(2)}, u32[]{:S(2)}) async-start(bf16[4,4,4096]{2,1,0:T(4,128)(2,1)} %reshape.157), calls=%async_computation.2 | async-start | bytes 262144 | tf_op jit(solution)/shard_map/all_to_all | solution.py:22
  749.3 8.1 %copy-start.2 = (f32[128,1,4096]{2,1,0:T(1,128)S(1)}, f32[128,1,4096]{2,1,0:T(1,128)}, u32[]{:S(2)}) copy-start(f32[128,1,4096]{2,1,0:T(1,128)} %get-tuple-element.5) | copy-start | bytes 6291460
  749.3 8.1 %copy-start.3 = (f32[128,1,4096]{2,1,0:T(1,128)S(1)}, f32[128,1,4096]{2,1,0:T(1,128)}, u32[]{:S(2)}) copy-start(f32[128,1,4096]{2,1,0:T(1,128)} %get-tuple-element.6) | copy-start | bytes 6291460
  760.6 5.0 copy-start.1
Sparse Core Ops, SparseCore 0:
  32.4 138.2 all-gather.2
  172.9 156.2 all-gather.4
  339.4 176.4 reduce-scatter.4
  518.2 174.4 reduce-scatter.2
where the time goes:
time: 780 us; the launch traced here: 772 us
  waiting for transfers between devices  570 us (73%)
  local copies, waits for them, and re-layouts  61.2 us (8%)
  starting transfers between devices  54.9 us (7%)
  matrix products  33.1 us (4%)
  blocking collectives  20.8 us (3%)
  other arithmetic  18.1 us (2%)
  between operations  14.2 us (2%)
    all_gather x2, waiting for transfers between devices, deliver(): gathered = lax.all_gather(own_rows, 'ep', axis=0, tiled=True)  263 us
    reduce_scatter x1, waiting for transfers between devices, local(): lax.psum_scatter(first + jnp.einsum('rf,df->rd', d_up, w_up[0], preferred...  163 us
    reduce_scatter x1, waiting for transfers between devices, local(): lax.psum_scatter(jnp.dot(hidden, w_down[0], preferred_element_type=jnp.fl...  143 us
    all_to_all x2, starting transfers between devices, give_back(): lax.all_to_all(results.reshape(n_rep, CAP, results.shape[1]), 'rep', spli...  54.1 us
    all_to_all x2, blocking collectives, deliver(): lax.all_to_all(buffer.reshape(n_rep, CAP, width), 'rep', split_axis=0, co...  20.8 us
  transfers between devices with their start and end apart: 6, of which 4 were waited for; matrix products, arithmetic and copies ran while one was open for 8% of the time, Pallas kernels for 0%

commit v1 on v0

v1 whole, which is shorter than its diff:
```python
import functools

import jax
import jax.numpy as jnp
from jax import lax
from jax.experimental import pallas as pl
from jax.experimental.pallas import tpu as pltpu
from jax.sharding import PartitionSpec as P

MESH = pl.DeviceIdType.MESH
F32, BF16 = jnp.float32, jnp.bfloat16
D, FF, TOK, SLOT = 4096, 256, 128, 16
QUARTER = D // 4
SIZES = {"z": 4, "y": 2, "x": 4}
PARTS = (
    (0, 1408, "yzx"),
    (1408, 2816, "yxz"),
    (2816, 3456, "zxy"),
    (3456, 4096, "xzy"),
)
COPIES = 200


def dot(a, b, ca=1, cb=0):
    return lax.dot_general(a, b, (((ca,), (cb,)), ((), ())), preferred_element_type=F32)


def stages(part):
    order = part[2]
    for s, axis in enumerate(order):
        free = order[:s]
        halved = "y" if "y" in free else (free[0] if free else None)
        yield axis, free, halved


def kernel(
    ids_ref, wts_ref, tok_hbm, cot_hbm, wg_hbm, wu_hbm, wd_hbm,
    mixed_hbm, gtok_hbm, gg_hbm, gu_hbm, gd_hbm,
    tok, cot, wg, wu, wd, xs, us, ps, qs, act, fac, hid, dgu, gg, gu, gd,
    out_m, out_g, box_s, box_r, local_sem, send_sem, recv_sem, *landing,
):
    ep, rep = lax.axis_index("ep"), lax.axis_index("rep")
    own = {"z": ep // 8, "y": (ep // 4) % 2, "x": ep % 4}
    half, core = rep // 2, rep % 2

    def place(z=None, y=None, x=None, h=None, c=None):
        z, y, x = (own[k] if v is None else v for k, v in (("z", z), ("y", y), ("x", x)))
        return (z * 8 + y * 4 + x, (half if h is None else h) * 2 + (core if c is None else c))

    after = {a: (own[a] + 1) % SIZES[a] for a in SIZES}
    before = {a: (own[a] + SIZES[a] - 1) % SIZES[a] for a in SIZES}
    far = {a: (own[a] + 2) % SIZES[a] for a in SIZES}

    def fetch(src, dst, i):
        copy = pltpu.make_async_copy(src, dst, local_sem.at[i])
        copy.start()
        return copy

    get_tok = fetch(tok_hbm, tok, 0)
    get_cot = fetch(cot_hbm, cot, 1)
    get_w = [fetch(wg_hbm.at[0], wg, 2), fetch(wu_hbm.at[0], wu, 3), fetch(wd_hbm.at[0], wd, 4)]

    traders = [place(c=1 - core), place(y=1 - own["y"], h=1 - half), place(y=1 - own["y"], h=1 - half, c=1 - core)]
    neighbours = traders + [place(y=1 - own["y"])]
    for a in "zx":
        neighbours += [place(**{a: after[a]}), place(**{a: before[a]})]
    barrier = pltpu.get_barrier_semaphore()
    for device in neighbours:
        pl.semaphore_signal(barrier, inc=1, device_id=device, device_id_type=MESH)

    sent = []

    def send(src, dst, device):
        i = len(sent)
        copy = pltpu.make_async_remote_copy(
            src, dst, send_sem.at[i], recv_sem.at[i], device_id=device, device_id_type=MESH
        )
        copy.start()
        sent.append(copy)
        return copy

    ids = ids_ref[...].astype(F32)
    wts = wts_ref[...]
    along = [jnp.broadcast_to(ids[:, k : k + 1], (TOK, TOK)).T[:64] for k in range(2)]
    w_along = [jnp.broadcast_to(wts[:, k : k + 1], (TOK, TOK)).T[:64] for k in range(2)]
    row = lax.broadcasted_iota(jnp.int32, (64, TOK), 0)
    expert, quarter, spot = row // 16, (row // 4) % 4, (row % 4).astype(F32)
    one = [jnp.where(a == expert.astype(F32), 1.0, 0.0).astype(F32) for a in along]
    hit = one[0] + one[1]
    t0 = lax.broadcasted_iota(jnp.int32, (TOK, TOK), 0)
    t1 = lax.broadcasted_iota(jnp.int32, (TOK, TOK), 1)
    earlier = dot(hit.astype(BF16), jnp.where(t0 < t1, 1.0, 0.0).astype(BF16))
    taken = jnp.where(earlier == spot, hit, 0.0)
    row_weight = jnp.sum(taken * (one[0] * w_along[0] + one[1] * w_along[1]), axis=1, keepdims=True)
    pick = [jnp.where(quarter == q, taken, 0.0).astype(BF16) for q in range(4)]

    def pack(values):
        return sum(dot(pick[q], values[:, q * QUARTER : (q + 1) * QUARTER]) for q in range(4))

    def trade(n):
        copies = [send(box_s.at[n, d[1]], box_r.at[n, rep], d) for d in traders]
        box_r[n, rep] = box_s[n, rep]
        return copies

    get_tok.wait()
    box_s[0] = pack(tok[...]).astype(BF16).reshape(4, 16, QUARTER)
    pl.semaphore_wait(barrier, len(neighbours))
    trade_x = trade(0)
    get_cot.wait()
    box_s[1] = (pack(cot[...]) * row_weight).astype(BF16).reshape(4, 16, QUARTER)
    trade_u = trade(1)

    def settle(copies, n, buf):
        for copy in copies:
            copy.wait_recv()
        r = lax.broadcasted_iota(jnp.int32, (16, 64), 0)
        s = lax.broadcasted_iota(jnp.int32, (16, 64), 1)
        blocks = box_r[n].reshape(64, QUARTER)
        for q in range(4):
            turn = jnp.where(s == (r // 4) * 16 + q * 4 + r % 4, 1.0, 0.0).astype(BF16)
            buf[own["z"], own["y"], own["x"], :, q * QUARTER : (q + 1) * QUARTER] = dot(turn, blocks).astype(BF16)

    def region(part, axis, at, free, halved, which=None):
        lo, hi, _ = part
        index = []
        for a in "zyx":
            if a == axis:
                index.append(pl.ds(at, 1))
            elif a in free:
                n = SIZES[a]
                if which is None or a != halved:
                    index.append(pl.ds(0, n))
                else:
                    index.append(pl.ds(which * (n // 2), n // 2))
            else:
                index.append(pl.ds(own[a], 1))
        if which is not None and halved is None:
            cut = lo + 384
            lo, hi = (lo, cut) if which == 0 else (cut, hi)
        return (*index, slice(None), pl.ds(lo, hi - lo))

    def within(part, free, halved, which):
        lo, hi, _ = part
        index = [
            pl.ds(which * (SIZES[a] // 2), SIZES[a] // 2) if a == halved else slice(None) for a in "zyx"
        ]
        cols = slice(None)
        if halved is None:
            cols = pl.ds(0, 384) if which == 0 else pl.ds(384, hi - lo - 384)
        return (*index, slice(None), cols)

    def gather(part, buf):
        for axis, free, halved in stages(part):
            mine = buf.at[region(part, axis, own[axis], free, halved)]
            up, down = place(**{axis: after[axis]}), place(**{axis: before[axis]})
            if SIZES[axis] == 2:
                copy = send(mine, mine, up)
                yield
                copy.wait_recv()
                continue
            a, b = send(mine, mine, up), send(mine, mine, down)
            yield
            a.wait_recv()
            r = buf.at[region(part, axis, before[axis], free, halved, 0)]
            a = send(r, r, up)
            b.wait_recv()
            r = buf.at[region(part, axis, after[axis], free, halved, 1)]
            b = send(r, r, down)
            yield
            a.wait_recv()
            b.wait_recv()

    landing = list(landing)

    def scatter(part, buf):
        shapes = landings(part)
        spare = iter(landing[: len(shapes)])
        del landing[: len(shapes)]
        return walk_back(part, buf, spare)

    def walk_back(part, buf, spare):
        for axis, free, halved in reversed(list(stages(part))):
            up, down = place(**{axis: after[axis]}), place(**{axis: before[axis]})
            mine = region(part, axis, own[axis], free, halved)
            if SIZES[axis] == 2:
                land = next(spare)
                copy = send(buf.at[region(part, axis, after[axis], free, halved)], land, up)
                yield
                copy.wait_recv()
                buf[mine] = (buf[mine].astype(F32) + land[...].astype(F32)).astype(BF16)
                continue
            via_l, via_r, land_l, land_r = next(spare), next(spare), next(spare), next(spare)
            half0, half1 = (within(part, free, halved, w) for w in (0, 1))
            o0 = send(buf.at[region(part, axis, far[axis], free, halved, 0)], via_l, up)
            o1 = send(buf.at[region(part, axis, far[axis], free, halved, 1)], via_r, down)
            e1 = send(buf.at[region(part, axis, after[axis], free, halved, 1)], land_l.at[half1], up)
            e0 = send(buf.at[region(part, axis, before[axis], free, halved, 0)], land_r.at[half0], down)
            yield
            o0.wait_recv()
            r = region(part, axis, after[axis], free, halved, 0)
            buf[r] = (buf[r].astype(F32) + via_l[...].astype(F32)).astype(BF16)
            f0 = send(buf.at[r], land_l.at[half0], up)
            o1.wait_recv()
            r = region(part, axis, before[axis], free, halved, 1)
            buf[r] = (buf[r].astype(F32) + via_r[...].astype(F32)).astype(BF16)
            f1 = send(buf.at[r], land_r.at[half1], down)
            yield
            for copy in (e1, e0, f0, f1):
                copy.wait_recv()
            buf[mine] = (buf[mine].astype(F32) + land_l[...].astype(F32) + land_r[...].astype(F32)).astype(BF16)

    def go(walks, which=(0, 1, 2, 3)):
        for w in which:
            next(walks[w], None)

    def rows(i):
        return pl.ds(pl.multiple_of(i * 256, 256), 256)

    def forward():
        @pl.loop(0, 2)
        def _(i):
            z = pl.ds(i * 2, 2)
            x = xs[z].reshape(256, D)
            g = dot(x, wg[...])
            u = dot(x, wu[...])
            s = 1.0 / (1.0 + jnp.exp(-g))
            a = g * s
            h = (a * u).astype(BF16)
            act[rows(i), :] = a
            fac[rows(i), :] = u * s * (1.0 + g * (1.0 - s))
            hid[rows(i), :] = h

            @pl.loop(0, 8)
            def _(n):
                cols = pl.ds(pl.multiple_of(n * 512, 512), 512)
                ps[z, :, :, :, cols] = dot(h, wd[:, cols]).astype(BF16).reshape(2, 2, 4, SLOT, 512)

    def backward():
        @pl.loop(0, 2)
        def _(i):
            d = dot(us[pl.ds(i * 2, 2)].reshape(256, D), wd[...], 1, 1)
            dgu[rows(i), 0:FF] = (d * fac[rows(i), :]).astype(BF16)
            dgu[rows(i), FF : 2 * FF] = (d * act[rows(i), :]).astype(BF16)

    def row_grads():
        @pl.loop(0, 2)
        def _(i):
            dg, du = dgu[rows(i), 0:FF], dgu[rows(i), FF : 2 * FF]

            @pl.loop(0, 8)
            def _(n):
                cols = pl.ds(pl.multiple_of(n * 512, 512), 512)
                g = dot(dg, wg[cols, :], 1, 1) + dot(du, wu[cols, :], 1, 1)
                qs[pl.ds(i * 2, 2), :, :, :, cols] = g.astype(BF16).reshape(2, 2, 4, SLOT, 512)

    def grad_in():
        @pl.loop(0, 8)
        def _(n):
            cols = pl.ds(pl.multiple_of(n * 512, 512), 512)
            g = dot(xs[:, :, :, :, cols].reshape(512, 512), dgu[...], 0, 0)
            gg[cols, :] = g[:, 0:FF].astype(BF16)
            gu[cols, :] = g[:, FF : 2 * FF].astype(BF16)

        return [fetch(gg, gg_hbm.at[0], 5), fetch(gu, gu_hbm.at[0], 6)]

    def grad_out():
        @pl.loop(0, 8)
        def _(n):
            cols = pl.ds(pl.multiple_of(n * 512, 512), 512)
            gd[:, cols] = dot(hid[...], us[:, :, :, :, cols].reshape(512, 512), 0, 0).astype(BF16)

        return [fetch(gd, gd_hbm.at[0], 7)]

    def send_back(n, buf):
        r = lax.broadcasted_iota(jnp.int32, (64, 16), 0)
        s = lax.broadcasted_iota(jnp.int32, (64, 16), 1)
        total = 0.0
        for q in range(4):
            turn = jnp.where((s == (r // 16) * 4 + r % 4) & ((r // 4) % 4 == q), 1.0, 0.0).astype(BF16)
            total += dot(turn, buf[own["z"], own["y"], own["x"], :, q * QUARTER : (q + 1) * QUARTER])
        box_s[n] = total.astype(BF16).reshape(4, 16, QUARTER)
        return trade(n)

    col = lax.broadcasted_iota(jnp.int32, (TOK, 64), 1)
    c_expert, c_quarter, c_spot = (col // 16).astype(F32), (col // 4) % 4, (col % 4).astype(F32)
    two = [jnp.where(jnp.broadcast_to(ids[:, k : k + 1], (TOK, 64)) == c_expert, 1.0, 0.0) for k in range(2)]
    c_earlier = dot(jnp.where(t1 < t0, 1.0, 0.0).astype(BF16), (two[0] + two[1]).astype(BF16))
    two = [jnp.where(c_earlier == c_spot, m, 0.0) for m in two]

    def spread(m, q, n):
        return dot(jnp.where(c_quarter == q, m, 0.0).astype(BF16), box_r[n].reshape(64, QUARTER))

    settle(trade_x, 0, xs)
    xw = [gather(part, xs) for part in PARTS]
    go(xw)
    settle(trade_u, 1, us)
    uw = [gather(part, us) for part in PARTS]
    go(uw)
    go(xw)
    go(xw)
    go(uw)
    go(xw)
    go(uw)
    go(xw, (2, 3, 0, 1))
    go(uw)
    go(xw)
    go(uw, (2, 3))
    for copy in get_w:
        copy.wait()
    forward()
    pw = [scatter(part, ps) for part in PARTS]
    go(uw, (0, 1))
    go(pw)
    go(uw)
    backward()
    go(pw)
    row_grads()
    qw = [scatter(part, qs) for part in PARTS]
    go(qw)
    go(pw)
    go(pw)
    go(qw)
    go(pw)
    outs = grad_in()
    go(qw)
    go(pw)
    trade_m = send_back(2, ps)
    outs += grad_out()
    go(qw)
    for copy in trade_m:
        copy.wait_recv()
    for q in range(4):
        cols = slice(q * QUARTER, (q + 1) * QUARTER)
        out_m[:, cols] = (wts[:, 0:1] * spread(two[0], q, 2) + wts[:, 1:2] * spread(two[1], q, 2)).astype(BF16)
    outs.append(fetch(out_m, mixed_hbm, 8))
    go(qw)
    go(qw)
    trade_g = send_back(3, qs)
    for copy in trade_g:
        copy.wait_recv()
    for q in range(4):
        cols = slice(q * QUARTER, (q + 1) * QUARTER)
        out_g[:, cols] = spread(two[0] + two[1], q, 3).astype(BF16)
    outs.append(fetch(out_g, gtok_hbm, 9))
    for copy in sent:
        copy.wait_send()
    for copy in outs:
        copy.wait()


def landings(part):
    width, shapes = part[1] - part[0], []
    for axis, free, halved in reversed(list(stages(part))):
        whole = tuple(SIZES[a] if a in free else 1 for a in "zyx")
        if SIZES[axis] == 2:
            shapes.append((*whole, SLOT, width))
            continue
        cut = tuple(n // 2 if a == halved else n for a, n in zip("zyx", whole))
        widths = (384, width - 384) if halved is None else (width, width)
        shapes += [(*cut, SLOT, w) for w in widths] + [(*whole, SLOT, width)] * 2
    return shapes


def local(tokens, expert_ids, route_weights, w_gate, w_up, w_down, cotangent):
    vm = lambda *shape, dtype=BF16: pltpu.VMEM(shape, dtype)
    grid5 = (4, 2, 4, SLOT, D)
    scratch = [
        vm(TOK, D), vm(TOK, D), vm(D, FF), vm(D, FF), vm(FF, D),
        vm(*grid5), vm(*grid5), vm(*grid5), vm(*grid5),
        vm(512, FF, dtype=F32), vm(512, FF, dtype=F32), vm(512, FF), vm(512, 2 * FF),
        vm(D, FF), vm(D, FF), vm(FF, D), vm(TOK, D), vm(TOK, D),
        vm(4, 4, 16, QUARTER), vm(4, 4, 16, QUARTER),
        pltpu.SemaphoreType.DMA((10,)),
        pltpu.SemaphoreType.DMA((COPIES,)),
        pltpu.SemaphoreType.DMA((COPIES,)),
    ]
    scratch += [vm(*s) for _ in range(2) for part in PARTS for s in landings(part)]
    any_spec = pl.BlockSpec(memory_space=pl.ANY)
    vmem_spec = pl.BlockSpec(memory_space=pltpu.VMEM)
    shape = jax.ShapeDtypeStruct
    return pl.pallas_call(
        kernel,
        out_shape=(
            shape((TOK, D), BF16), shape((TOK, D), BF16),
            shape((1, D, FF), BF16), shape((1, D, FF), BF16), shape((1, FF, D), BF16),
        ),
        in_specs=[vmem_spec] * 2 + [any_spec] * 5,
        out_specs=(any_spec,) * 5,
        scratch_shapes=scratch,
        compiler_params=pltpu.CompilerParams(
            collective_id=0, has_side_effects=True, vmem_limit_bytes=60 << 20
        ),
        cost_estimate=pl.CostEstimate(
            flops=9 * 2 * 512 * D * FF, bytes_accessed=16 << 20, transcendentals=512 * FF
        ),
        name="moe",
    )(expert_ids, route_weights, tokens, cotangent, w_gate, w_up, w_down)


def solution(mesh):
    rows, up, down = P(("ep", "rep"), None), P("rep", None, "ep"), P("rep", "ep", None)
    return jax.shard_map(
        local,
        mesh=mesh,
        in_specs=(rows, rows, rows, up, up, down, rows),
        out_specs=(rows, rows, up, up, down),
        check_vma=False,
    )
```

time: 780 us -> 141 us (0.18)
  waiting for transfers between devices: 570 us -> 0 us
  Pallas kernels: 0 us -> 127 us
  starting transfers between devices: 54.9 us -> 0 us
  local copies, waits for them, and re-layouts: 61.2 us -> 12.3 us
  matrix products: 33.1 us -> 0 us
  blocking collectives: 20.8 us -> 0 us
  other arithmetic: 18.1 us -> 0 us
  between operations: 14.2 us -> 0.66 us
    reduce_scatter x2 -> x0, waiting for transfers between devices: 307 us -> none  [the longest x1 163 us: local(): lax.psum_scatter(first + jnp.einsum('rf,df->rd', d_up, w_up[0], preferred...]
    all_gather x2 -> x0, waiting for transfers between devices: 263 us -> none  [deliver(): gathered = lax.all_gather(own_rows, 'ep', axis=0, tiled=True)]
    pallas_call x0 -> x1, Pallas kernels: none -> 127 us  [local(): pl.pallas_call(kernel, out_shape=(shape((TOK, D), BF16), shape((TOK, D),...]
    all_to_all x2 -> x0, starting transfers between devices: 54.1 us -> none  [give_back(): lax.all_to_all(results.reshape(n_rep, CAP, results.shape[1]), 'rep', spli...]
    dot_general x9 -> x0, matrix products: 33.1 us -> none  [the longest x1 4.98 us: local(): jnp.einsum('rf,rd->fd', hidden, upstream_rows, preferred_element_type=jnp...]
    all_to_all x2 -> x0, blocking collectives: 20.8 us -> none  [deliver(): lax.all_to_all(buffer.reshape(n_rep, CAP, width), 'rep', split_axis=0, co...]
    slice x6 -> x0, local copies, waits for them, and re-layouts: 18.1 us -> none  [the longest x1 9.85 us: local(): grad_tokens = (collected[:, 0] + collected[:, 1]).astype(jnp.bfloat16)]
    convert_element_type x2 -> x0, local copies, waits for them, and re-layouts: 11.1 us -> none  [unpack(): return padded[slot].astype(jnp.float32).reshape(tok_dev, 2, width)]
  transfers between devices with their start and end apart: 6 -> 0, of which waited for: 4 -> 0; matrix products, arithmetic and copies ran while one was open for 8% -> 0% of each run, Pallas kernels for 0% -> 0%
where the time goes in v1:
time: 141 us; the launch traced here: 140 us
  Pallas kernels  127 us (90%)
  local copies, waits for them, and re-layouts  12.3 us (9%)
    pallas_call x1, Pallas kernels, local(): pl.pallas_call(kernel, out_shape=(shape((TOK, D), BF16), shape((TOK, D),...  127 us
    unnamed x15, local copies, waits for them, and re-layouts  12.3 us

profile of v1, /device:TPU:1, one launch (start us, length us, event | category | flops | bytes accessed | tf_op | source)
XLA Modules:
  0.0 140.3 jit_solution(16276760811590161826)
XLA Ops:
  0.6 1.4 %copy.12.ids_ref = s32[128,2]{1,0:T(8,128)} copy(s32[128,2]{0,1:T(2,128)} %param.8) | data formatting | bytes 2048 | tf_op args[1]
  2.0 1.4 %copy.13.wts_ref = f32[128,2]{1,0:T(8,128)} copy(f32[128,2]{0,1:T(2,128)} %param.9) | data formatting | bytes 2048 | tf_op args[2]
  3.5 127.4 %moe.1 = (bf16[128,4096]{1,0:T(8,128)(2,1)}, bf16[128,4096]{1,0:T(8,128)(2,1)}, bf16[1,4096,256]{2,1,0:T(8,128)(2,1)}, bf16[1,4096,256]{2,1,0:T(8,128)(2,1)}, bf16[1,256,4096]{2,1,0:T(8,128)(2,1)}) custom-call(s32[128,2]{1,0:T(8,128)} %copy.12.ids_ref, f32[128,2]{1,0:T(8,128)} %copy.13.wts_ref, bf16[128,4096]{1,0:T(8,128)(2,1)} %tok_hbm.1, ...), custom_call_target="tpu_custom_call" | custom-call | flops 9663676416 | bytes 16777216 | tf_op jit(solution)/shard_map/moe/pallas_call | solution.py:381
  130.8 0.0 copy-start.3
  130.8 0.0 copy-start.2
  130.9 2.4 %copy.19 = bf16[128,4096]{1,0:T(8,128)(2,1)} copy(bf16[128,4096]{1,0:T(8,128)(2,1)} %get-tuple-element.10) | data formatting | bytes 2097152
  133.3 0.0 copy-done.3
  133.3 1.0 copy.20
  134.3 0.0 copy-done.2
  134.3 0.0 copy-start.1
  134.3 1.3 copy.21
  135.6 1.0 copy-done.1
  136.6 0.0 copy-start
  136.6 1.3 copy.22
  137.9 1.0 copy-done
  139.0 1.3 copy.23
Async XLA Ops:
  130.8 2.5 %copy-start.3 = (bf16[128,4096]{1,0:T(8,128)(2,1)S(1)}, bf16[128,4096]{1,0:T(8,128)(2,1)}, u32[]{:S(2)}) copy-start(bf16[128,4096]{1,0:T(8,128)(2,1)} %get-tuple-element.11) | copy-start | bytes 3145732
  130.8 3.4 %copy-start.2 = (bf16[1,4096,256]{2,1,0:T(8,128)(2,1)S(1)}, bf16[1,4096,256]{2,1,0:T(8,128)(2,1)}, u32[]{:S(2)}) copy-start(bf16[1,4096,256]{2,1,0:T(8,128)(2,1)} %get-tuple-element.12) | copy-start | bytes 6291460
  134.3 2.3 %copy-start.1 = (bf16[1,4096,256]{2,1,0:T(8,128)(2,1)S(1)}, bf16[1,4096,256]{2,1,0:T(8,128)(2,1)}, u32[]{:S(2)}) copy-start(bf16[1,4096,256]{2,1,0:T(8,128)(2,1)} %get-tuple-element.13) | copy-start | bytes 6291460
  136.6 2.3 %copy-start = (bf16[1,256,4096]{2,1,0:T(8,128)(2,1)S(1)}, bf16[1,256,4096]{2,1,0:T(8,128)(2,1)}, u32[]{:S(2)}) copy-start(bf16[1,256,4096]{2,1,0:T(8,128)(2,1)} %get-tuple-element.14) | copy-start | bytes 6291460

commit v2 on v1

v2 whole, which is shorter than its diff:
```python
import functools

import jax
import jax.numpy as jnp
from jax import lax
from jax.experimental import pallas as pl
from jax.experimental.pallas import tpu as pltpu
from jax.sharding import PartitionSpec as P

MESH = pl.DeviceIdType.MESH
F32, BF16 = jnp.float32, jnp.bfloat16
D, FF, TOK, SLOT = 4096, 256, 128, 16
QUARTER = D // 4
SIZES = {"z": 4, "y": 2, "x": 4}
PARTS = (
    (0, 1408, "yzx"),
    (1408, 2816, "yxz"),
    (2816, 3456, "zxy"),
    (3456, 4096, "xzy"),
)
LATE, CUT = 640, 384
COPIES = 340


def dot(a, b, ca=1, cb=0):
    return lax.dot_general(a, b, (((ca,), (cb,)), ((), ())), preferred_element_type=F32)


def kernel(
    ids_ref, wts_ref, tok_hbm, cot_hbm, wg_hbm, wu_hbm, wd_hbm,
    out_m, out_g, gg, gu, gd,
    tok, cot, wg, wu, wd, xs, us, ps, qs, act, fac, hid, dgu,
    box_s, box_r, local_sem, send_sem, recv_sem, *landing,
):
    ep, rep = lax.axis_index("ep"), lax.axis_index("rep")
    own = {"z": ep // 8, "y": (ep // 4) % 2, "x": ep % 4}
    half, core = rep // 2, rep % 2

    def place(z=None, y=None, x=None, h=None, c=None):
        z, y, x = (own[k] if v is None else v for k, v in (("z", z), ("y", y), ("x", x)))
        return (z * 8 + y * 4 + x, (half if h is None else h) * 2 + (core if c is None else c))

    after = {a: (own[a] + 1) % SIZES[a] for a in SIZES}
    before = {a: (own[a] + SIZES[a] - 1) % SIZES[a] for a in SIZES}
    far = {a: (own[a] + 2) % SIZES[a] for a in SIZES}

    def fetch(src, dst, i):
        copy = pltpu.make_async_copy(src, dst, local_sem.at[i])
        copy.start()
        return copy

    get_tok = fetch(tok_hbm, tok, 0)
    get_cot = fetch(cot_hbm, cot, 1)
    get_w = [fetch(wg_hbm.at[0], wg, 2), fetch(wu_hbm.at[0], wu, 3), fetch(wd_hbm.at[0], wd, 4)]

    traders = [place(c=1 - core), place(y=1 - own["y"], h=1 - half), place(y=1 - own["y"], h=1 - half, c=1 - core)]
    neighbours = traders + [place(y=1 - own["y"])]
    for a in "zx":
        neighbours += [place(**{a: after[a]}), place(**{a: before[a]})]
    barrier = pltpu.get_barrier_semaphore()
    for device in neighbours:
        pl.semaphore_signal(barrier, inc=1, device_id=device, device_id_type=MESH)

    sent = []

    def send(src, dst, device):
        i = len(sent)
        copy = pltpu.make_async_remote_copy(
            src, dst, send_sem.at[i], recv_sem.at[i], device_id=device, device_id_type=MESH
        )
        copy.start()
        sent.append(copy)
        return copy

    ids = [jnp.broadcast_to(ids_ref[k : k + 1, :].astype(F32), (TOK, TOK)) for k in range(2)]
    wts = [jnp.broadcast_to(wts_ref[k : k + 1, :], (TOK, TOK)) for k in range(2)]
    along, w_along = [a[:64] for a in ids], [w[:64] for w in wts]
    row = lax.broadcasted_iota(jnp.int32, (64, TOK), 0)
    expert, quarter, spot = row // 16, (row // 4) % 4, (row % 4).astype(F32)
    one = [jnp.where(a == expert.astype(F32), 1.0, 0.0).astype(F32) for a in along]
    hit = one[0] + one[1]
    t0 = lax.broadcasted_iota(jnp.int32, (TOK, TOK), 0)
    t1 = lax.broadcasted_iota(jnp.int32, (TOK, TOK), 1)
    earlier = dot(hit.astype(BF16), jnp.where(t0 < t1, 1.0, 0.0).astype(BF16))
    taken = jnp.where(earlier == spot, hit, 0.0)
    row_weight = jnp.sum(taken * (one[0] * w_along[0] + one[1] * w_along[1]), axis=1, keepdims=True)
    pick = [jnp.where(quarter == q, taken, 0.0).astype(BF16) for q in range(4)]

    def pack(values):
        return sum(dot(pick[q], values[:, q * QUARTER : (q + 1) * QUARTER]) for q in range(4))

    def trade(n):
        copies = [send(box_s.at[n, d[1]], box_r.at[n, rep], d) for d in traders]
        box_r[n, rep] = box_s[n, rep]
        return copies

    get_tok.wait()
    box_s[0] = pack(tok[...]).astype(BF16).reshape(4, 16, QUARTER)
    pl.semaphore_wait(barrier, len(neighbours))
    trade_x = trade(0)
    get_cot.wait()
    box_s[1] = (pack(cot[...]) * row_weight).astype(BF16).reshape(4, 16, QUARTER)
    trade_u = trade(1)

    def settle(copies, n, buf):
        for copy in copies:
            copy.wait_recv()
        r = lax.broadcasted_iota(jnp.int32, (16, 64), 0)
        s = lax.broadcasted_iota(jnp.int32, (16, 64), 1)
        blocks = box_r[n].reshape(64, QUARTER)
        for q in range(4):
            turn = jnp.where(s == (r // 4) * 16 + q * 4 + r % 4, 1.0, 0.0).astype(BF16)
            buf[own["z"], own["y"], own["x"], :, q * QUARTER : (q + 1) * QUARTER] = dot(turn, blocks).astype(BF16)

    def at(part, cut=None, **where):
        lo, hi = part[0], part[1]
        if cut is not None:
            lo, hi = (lo, lo + CUT) if cut == 0 else (lo + CUT, hi)
        index = [pl.ds(*where[a]) if a in where else pl.ds(own[a], 1) for a in "zyx"]
        return (*index, slice(None), pl.ds(lo, hi - lo))

    def all_of(axis):
        return (0, SIZES[axis])

    def sides(axis):
        return place(**{axis: after[axis]}), place(**{axis: before[axis]})

    def gather_y_first(part, buf):
        _, _, (_, a, b) = part
        (up_a, down_a), (up_b, down_b) = sides(a), sides(b)

        def push(where, device, y=(0, 2)):
            ref = buf.at[at(part, **where, y=y)]
            return send(ref, ref, device)

        def pass_on(up, down, where):
            up.wait_recv()
            up = push({**where, b: (before[b], 1)}, up_b, (0, 1))
            down.wait_recv()
            return up, push({**where, b: (after[b], 1)}, down_b, (1, 1))

        ref = buf.at[at(part)]
        y = send(ref, ref, sides("y")[0])
        yield
        y.wait_recv()
        au, ad = push({}, up_a), push({}, down_a)
        x0 = push({}, up_b), push({}, down_b)
        yield
        low, high, other = {a: (before[a], 1)}, {a: (after[a], 1)}, {a: (far[a], 1)}
        au.wait_recv()
        au = push(low, up_a, (0, 1))
        ad.wait_recv()
        ad = push(high, down_a, (1, 1))
        x1 = push(low, up_b), push(low, down_b)
        x2 = push(high, up_b), push(high, down_b)
        yield
        ends = [*pass_on(*x0, {})]
        yield
        au.wait_recv()
        ad.wait_recv()
        x3 = push(other, up_b), push(other, down_b)
        yield
        ends += [*pass_on(*x1, low), *pass_on(*x2, high)]
        yield
        ends += [*pass_on(*x3, other)]
        yield
        for copy in ends:
            copy.wait_recv()

    def gather_y_last(part, buf):
        _, _, (a, b, _) = part
        (up_a, down_a), (up_b, down_b) = sides(a), sides(b)
        over = sides("y")[0]

        def push(where, device, cut=None):
            ref = buf.at[at(part, cut, **where)]
            return send(ref, ref, device)

        au, ad = push({}, up_a), push({}, down_a)
        yield
        au.wait_recv()
        au = push({a: (before[a], 1)}, up_a, 0)
        ad.wait_recv()
        ad = push({a: (after[a], 1)}, down_a, 1)
        yield
        au.wait_recv()
        ad.wait_recv()
        whole = {a: all_of(a)}
        bu, bd = push(whole, up_b), push(whole, down_b)
        ends = [push(whole, over)]
        yield
        bu.wait_recv()
        bu = push({a: (0, 2), b: (before[b], 1)}, up_b)
        bd.wait_recv()
        bd = push({a: (2, 2), b: (after[b], 1)}, down_b)
        ends += [push({**whole, b: (before[b], 1)}, over), push({**whole, b: (after[b], 1)}, over)]
        yield
        bu.wait_recv()
        bd.wait_recv()
        ends += [push({**whole, b: (far[b], 1)}, over)]
        yield
        for copy in ends:
            copy.wait_recv()

    def gather(part, buf):
        return (gather_y_first if part[2][0] == "y" else gather_y_last)(part, buf)

    def add(buf, index, *landed):
        total = buf[index].astype(F32)
        for ref in landed:
            total += ref[...].astype(F32)
        buf[index] = total.astype(BF16)

    landing = list(landing)

    class Ring:
        def __init__(self, part, buf, axis, split, where):
            self.up, self.down = sides(axis)
            self.axis, self.buf, self.where = axis, buf, where
            self.via = [landing.pop(0) for _ in range(2)]
            self.land = [landing.pop(0) for _ in range(2)]
            self.half = [(lambda p, i=i: at(part, **{**where, axis: (p, 1)}, **split(i)[0])) for i in range(2)]
            self.part_of = [split(i)[1] for i in range(2)]

        def far(self):
            p = far[self.axis]
            self.o0 = send(self.buf.at[self.half[0](p)], self.via[0], self.up)
            self.o1 = send(self.buf.at[self.half[1](p)], self.via[1], self.down)

        def near_up(self):
            ref = self.buf.at[self.half[1](after[self.axis])]
            self.e1 = send(ref, self.land[0].at[self.part_of[1]], self.up)

        def near_down(self):
            ref = self.buf.at[self.half[0](before[self.axis])]
            self.e0 = send(ref, self.land[1].at[self.part_of[0]], self.down)

        def start(self):
            self.far()
            self.near_up()
            self.near_down()

        def middle(self):
            self.o0.wait_recv()
            index = self.half[0](after[self.axis])
            add(self.buf, index, self.via[0])
            self.f0 = send(self.buf.at[index], self.land[0].at[self.part_of[0]], self.up)
            self.o1.wait_recv()
            index = self.half[1](before[self.axis])
            add(self.buf, index, self.via[1])
            self.f1 = send(self.buf.at[index], self.land[1].at[self.part_of[1]], self.down)

        def end(self, index):
            for copy in (self.e1, self.e0, self.f0, self.f1):
                copy.wait_recv()
            add(self.buf, index, *self.land)

    def by_y(i):
        return {"y": (i, 1)}, (slice(None), pl.ds(i, 1))

    def by_columns(i):
        return {"cut": i}, (slice(None),) * 4 + ((pl.ds(0, CUT), pl.ds(CUT, LATE - CUT))[i],)

    def by_place(axis):
        def split(i):
            here = pl.ds(2 * i, 2)
            return {axis: (2 * i, 2)}, (here,) if axis == "z" else (slice(None), slice(None), here)

        return split

    def scatter_y_last(part, buf):
        _, _, (_, a, b) = part
        spots = {"far": (far[a], 1), "low": (before[a], 1), "high": (after[a], 1), "own": (own[a], 1)}
        rings = {k: Ring(part, buf, b, by_y, {a: spots[k]}) for k in ("far", "low", "high", "own")}
        last = Ring(part, buf, a, by_y, {})
        land_y = landing.pop(0)

        def finish(k):
            rings[k].end(at(part, **{a: spots[k]}, y=(0, 2)))

        def walk():
            rings["far"].start()
            rings["low"].start()
            yield
            rings["far"].middle()
            rings["high"].start()
            yield
            rings["low"].middle()
            finish("far")
            last.far()
            rings["own"].start()
            yield
            rings["high"].middle()
            finish("low")
            last.near_down()
            yield
            rings["own"].middle()
            finish("high")
            last.near_up()
            last.middle()
            yield
            finish("own")
            last.end(at(part, y=(0, 2)))
            y = send(buf.at[at(part, y=(after["y"], 1))], land_y, sides("y")[0])
            yield
            y.wait_recv()
            add(buf, at(part), land_y)

        return walk()

    def scatter_y_first(part, buf):
        _, _, (a, b, _) = part
        whole = {a: all_of(a)}
        spots = [{**whole, b: (p[b], 1)} for p in (far, before, after, own)]
        land_y = [landing.pop(0) for _ in spots]
        ring = Ring(part, buf, b, by_place(a), {})
        last = Ring(part, buf, a, by_columns, {})

        def walk():
            copies = [
                send(buf.at[at(part, **spot, y=(after["y"], 1))], land, sides("y")[0])
                for spot, land in zip(spots, land_y)
            ]

            def take(i):
                copies[i].wait_recv()
                add(buf, at(part, **spots[i]), land_y[i])

            yield
            take(0)
            ring.far()
            yield
            take(1)
            take(2)
            ring.near_down()
            ring.near_up()
            yield
            take(3)
            ring.middle()
            yield
            ring.end(at(part, **whole))
            last.start()
            yield
            last.middle()
            yield
            last.end(at(part))

        return walk()

    def scatter(part, buf):
        return (scatter_y_last if part[2][0] == "y" else scatter_y_first)(part, buf)

    def go(walks, which=(0, 1, 2, 3)):
        for w in which:
            next(walks[w], None)

    def rows(i):
        return pl.ds(i * 256, 256)

    def forward(i):
        z = pl.ds(i * 2, 2)
        x = xs[z].reshape(256, D)
        g = dot(x, wg[...])
        u = dot(x, wu[...])
        s = 1.0 / (1.0 + jnp.exp(-g))
        a = g * s
        h = (a * u).astype(BF16)
        act[rows(i), :] = a
        fac[rows(i), :] = u * s * (1.0 + g * (1.0 - s))
        hid[rows(i), :] = h

        @pl.loop(0, 8)
        def _(n):
            cols = pl.ds(pl.multiple_of(n * 512, 512), 512)
            ps[z, :, :, :, cols] = dot(h, wd[:, cols]).astype(BF16).reshape(2, 2, 4, SLOT, 512)

    def backward(i):
        d = dot(us[pl.ds(i * 2, 2)].reshape(256, D), wd[...], 1, 1)
        dgu[rows(i), 0:FF] = (d * fac[rows(i), :]).astype(BF16)
        dgu[rows(i), FF : 2 * FF] = (d * act[rows(i), :]).astype(BF16)

    def row_grads(i):
        dg, du = dgu[rows(i), 0:FF], dgu[rows(i), FF : 2 * FF]

        @pl.loop(0, 8)
        def _(n):
            cols = pl.ds(pl.multiple_of(n * 512, 512), 512)
            g = dot(dg, wg[cols, :], 1, 1) + dot(du, wu[cols, :], 1, 1)
            qs[pl.ds(i * 2, 2), :, :, :, cols] = g.astype(BF16).reshape(2, 2, 4, SLOT, 512)

    def grad_in(i):
        @pl.loop(4 * i, 4 * i + 4)
        def _(n):
            cols = pl.ds(pl.multiple_of(n * 512, 512), 512)
            g = dot(xs[:, :, :, :, cols].reshape(512, 512), dgu[...], 0, 0)
            gg[cols, :] = g[:, 0:FF].astype(BF16)
            gu[cols, :] = g[:, FF : 2 * FF].astype(BF16)

    def grad_out():
        @pl.loop(0, 8)
        def _(n):
            cols = pl.ds(pl.multiple_of(n * 512, 512), 512)
            gd[:, cols] = dot(hid[...], us[:, :, :, :, cols].reshape(512, 512), 0, 0).astype(BF16)

    def send_back(n, buf):
        r = lax.broadcasted_iota(jnp.int32, (64, 16), 0)
        s = lax.broadcasted_iota(jnp.int32, (64, 16), 1)
        total = 0.0
        for q in range(4):
            turn = jnp.where((s == (r // 16) * 4 + r % 4) & ((r // 4) % 4 == q), 1.0, 0.0).astype(BF16)
            total += dot(turn, buf[own["z"], own["y"], own["x"], :, q * QUARTER : (q + 1) * QUARTER])
        box_s[n] = total.astype(BF16).reshape(4, 16, QUARTER)
        return trade(n)

    col = lax.broadcasted_iota(jnp.int32, (TOK, 64), 1)
    c_expert, c_quarter, c_spot = (col // 16).astype(F32), (col // 4) % 4, (col % 4).astype(F32)
    two = [jnp.where(ids[k].T[:, :64] == c_expert, 1.0, 0.0) for k in range(2)]
    weight = [wts[k].T[:, 0:1] for k in range(2)]
    c_earlier = dot(jnp.where(t1 < t0, 1.0, 0.0).astype(BF16), (two[0] + two[1]).astype(BF16))
    two = [jnp.where(c_earlier == c_spot, m, 0.0) for m in two]

    def spread(m, q, n):
        return dot(jnp.where(c_quarter == q, m, 0.0).astype(BF16), box_r[n].reshape(64, QUARTER))

    settle(trade_x, 0, xs)
    xw = [gather(part, xs) for part in PARTS]
    go(xw)
    settle(trade_u, 1, us)
    uw = [gather(part, us) for part in PARTS]
    go(uw)
    go(xw)
    go(xw)
    go(uw)
    go(xw)
    go(xw)
    go(uw)
    go(xw)
    go(uw)
    go(xw)
    go(uw)
    go(xw)
    for copy in get_w:
        copy.wait()
    forward(0)
    go(uw)
    forward(1)
    go(uw)
    pw = [scatter(part, ps) for part in PARTS]
    qw = [scatter(part, qs) for part in PARTS]
    go(pw)
    go(uw)
    go(pw)
    backward(0)
    go(pw)
    backward(1)
    go(pw)
    row_grads(0)
    go(pw)
    row_grads(1)
    go(qw)
    go(pw)
    go(qw)
    grad_in(0)
    go(pw)
    trade_m = send_back(2, ps)
    go(qw)
    grad_in(1)
    go(qw)
    grad_out()
    go(qw)
    for copy in trade_m:
        copy.wait_recv()
    for q in range(4):
        cols = slice(q * QUARTER, (q + 1) * QUARTER)
        out_m[:, cols] = (weight[0] * spread(two[0], q, 2) + weight[1] * spread(two[1], q, 2)).astype(BF16)
    go(qw)
    go(qw)
    trade_g = send_back(3, qs)
    for copy in trade_g:
        copy.wait_recv()
    for q in range(4):
        cols = slice(q * QUARTER, (q + 1) * QUARTER)
        out_g[:, cols] = spread(two[0] + two[1], q, 3).astype(BF16)
    for copy in sent:
        copy.wait_send()


def landings(part):
    width, order = part[1] - part[0], part[2]

    def shape(cols=width, **sizes):
        return (*(sizes.get(a, 1) for a in "zyx"), SLOT, cols)

    if order[0] == "y":
        ring = [shape()] * 2 + [shape(y=2)] * 2
        return ring * 5 + [shape()]
    a = order[0]
    whole, cut = shape(**{a: 4}), shape(**{a: 2})
    return [whole] * 4 + [cut] * 2 + [whole] * 2 + [shape(CUT), shape(width - CUT)] + [shape()] * 2


def write_out(*refs):
    held, outs, sem = refs[:5], refs[5:10], refs[10]
    copies = [
        pltpu.make_async_copy(h, o if h.shape == o.shape else o.at[0], sem.at[i])
        for i, (h, o) in enumerate(zip(held, outs))
    ]
    for copy in copies:
        copy.start()
    for copy in copies:
        copy.wait()


def local(tokens, expert_ids, route_weights, w_gate, w_up, w_down, cotangent):
    vm = lambda *shape, dtype=BF16: pltpu.VMEM(shape, dtype)
    grid5 = (4, 2, 4, SLOT, D)
    scratch = [
        vm(TOK, D), vm(TOK, D), vm(D, FF), vm(D, FF), vm(FF, D),
        vm(*grid5), vm(*grid5), vm(*grid5), vm(*grid5),
        vm(512, FF, dtype=F32), vm(512, FF, dtype=F32), vm(512, FF), vm(512, 2 * FF),
        vm(4, 4, 16, QUARTER), vm(4, 4, 16, QUARTER),
        pltpu.SemaphoreType.DMA((5,)),
        pltpu.SemaphoreType.DMA((COPIES,)),
        pltpu.SemaphoreType.DMA((COPIES,)),
    ]
    scratch += [vm(*s) for _ in range(2) for part in PARTS for s in landings(part)]
    any_spec = pl.BlockSpec(memory_space=pl.ANY)
    vmem_spec = pl.BlockSpec(memory_space=pltpu.VMEM)
    shape = jax.ShapeDtypeStruct
    held = pl.pallas_call(
        kernel,
        out_shape=(
            vm(TOK, D), vm(TOK, D), vm(D, FF), vm(D, FF), vm(FF, D),
        ),
        in_specs=[vmem_spec] * 2 + [any_spec] * 5,
        out_specs=(vmem_spec,) * 5,
        scratch_shapes=scratch,
        compiler_params=pltpu.CompilerParams(
            collective_id=0, has_side_effects=True, vmem_limit_bytes=50 << 20
        ),
        cost_estimate=pl.CostEstimate(
            flops=9 * 2 * 512 * D * FF, bytes_accessed=16 << 20, transcendentals=512 * FF
        ),
        name="moe",
    )(expert_ids.T, route_weights.T, tokens, cotangent, w_gate, w_up, w_down)
    return pl.pallas_call(
        write_out,
        out_shape=(
            shape((TOK, D), BF16), shape((TOK, D), BF16),
            shape((1, D, FF), BF16), shape((1, D, FF), BF16), shape((1, FF, D), BF16),
        ),
        in_specs=[vmem_spec] * 5,
        out_specs=(any_spec,) * 5,
        scratch_shapes=[pltpu.SemaphoreType.DMA((5,))],
        compiler_params=pltpu.CompilerParams(vmem_limit_bytes=1 << 20),
        name="write_out",
    )(*(pltpu.with_memory_space_constraint(h, pltpu.VMEM) for h in held))


def solution(mesh):
    rows, up, down = P(("ep", "rep"), None), P("rep", None, "ep"), P("rep", "ep", None)
    return jax.shard_map(
        local,
        mesh=mesh,
        in_specs=(rows, rows, rows, up, up, down, rows),
        out_specs=(rows, rows, up, up, down),
        check_vma=False,
    )
```

time: 141 us -> 125 us (0.89)
  local copies, waits for them, and re-layouts: 12.3 us -> 0 us
  Pallas kernels: 127 us -> 124 us
    unnamed x15 -> x0, local copies, waits for them, and re-layouts: 12.3 us -> none
    pallas_call x1 -> x2, Pallas kernels: 127 us -> 124 us  [the longest x1 120 us: local(): pl.pallas_call(kernel, out_shape=(vm(TOK, D), vm(TOK, D), vm(D, FF), vm(D...]
where the time goes in v2:
time: 125 us
  Pallas kernels  124 us (99%)
    pallas_call x1, Pallas kernels, local(): pl.pallas_call(kernel, out_shape=(vm(TOK, D), vm(TOK, D), vm(D, FF), vm(D...  120 us
    pallas_call x1, Pallas kernels, local(): pl.pallas_call(write_out, out_shape=(shape((TOK, D), BF16), shape((TOK, D...  3.38 us

profile of v2, /device:TPU:1, one launch (start us, length us, event | category | flops | bytes accessed | tf_op | source)
XLA Modules:
  0.0 124.5 jit_solution(1621073278486811256)
XLA Ops:
  0.6 120.3 %moe.1 = (bf16[128,4096]{1,0:T(8,128)(2,1)S(1)}, bf16[128,4096]{1,0:T(8,128)(2,1)S(1)}, bf16[4096,256]{1,0:T(8,128)(2,1)S(1)}, bf16[4096,256]{1,0:T(8,128)(2,1)S(1)}, bf16[256,4096]{1,0:T(8,128)(2,1)S(1)}) custom-call(s32[2,128]{1,0:T(2,128)} %bitcast.2, f32[2,128]{1,0:T(2,128)} %bitcast.3, bf16[128,4096]{1,0:T(8,128)(2,1)} %tok_hbm.1, ...), custom_call_target="tpu_custom_call" | custom-call | flops 9663676416 | bytes 16777216 | tf_op jit(solution)/shard_map/moe/pallas_call | solution.py:530
  121.0 3.4 %write_out.1 = (bf16[128,4096]{1,0:T(8,128)(2,1)}, bf16[128,4096]{1,0:T(8,128)(2,1)}, bf16[1,4096,256]{2,1,0:T(8,128)(2,1)}, bf16[1,4096,256]{2,1,0:T(8,128)(2,1)}, bf16[1,256,4096]{2,1,0:T(8,128)(2,1)}) custom-call(bf16[128,4096]{1,0:T(8,128)(2,1)S(1)} %get-tuple-element.10.refs_0_, bf16[128,4096]{1,0:T(8,128)(2,1)S(1)} %get-tuple-element.11.refs_1_, ...), custom_call_target="tpu_custom_call" | custom-call | tf_op jit(solution)/shard_map/write_out/pallas_call | solution.py:546

commit v3 on v2

--- a/solution.py
+++ b/solution.py
@@ -1,4 +1,4 @@
-import functools
+import math
 
 import jax
 import jax.numpy as jnp
@@ -13,13 +13,13 @@
 QUARTER = D // 4
 SIZES = {"z": 4, "y": 2, "x": 4}
 PARTS = (
-    (0, 1408, "yzx"),
-    (1408, 2816, "yxz"),
-    (2816, 3456, "zxy"),
-    (3456, 4096, "xzy"),
+    (0, 1536, "yzx"),
+    (1536, 3072, "yxz"),
+    (3072, 3584, "zxy"),
+    (3584, 4096, "xzy"),
 )
-LATE, CUT = 640, 384
-COPIES = 340
+LATE, CUT = 512, 256
+ARRIVALS, DEPARTURES = 148, 20
 
 
 def dot(a, b, ca=1, cb=0):
@@ -51,7 +51,6 @@
 
     get_tok = fetch(tok_hbm, tok, 0)
     get_cot = fetch(cot_hbm, cot, 1)
-    get_w = [fetch(wg_hbm.at[0], wg, 2), fetch(wu_hbm.at[0], wu, 3), fetch(wd_hbm.at[0], wd, 4)]
 
     traders = [place(c=1 - core), place(y=1 - own["y"], h=1 - half), place(y=1 - own["y"], h=1 - half, c=1 - core)]
     neighbours = traders + [place(y=1 - own["y"])]
@@ -61,16 +60,30 @@
     for device in neighbours:
         pl.semaphore_signal(barrier, inc=1, device_id=device, device_id_type=MESH)
 
-    sent = []
-
-    def send(src, dst, device):
-        i = len(sent)
-        copy = pltpu.make_async_remote_copy(
-            src, dst, send_sem.at[i], recv_sem.at[i], device_id=device, device_id_type=MESH
-        )
-        copy.start()
-        sent.append(copy)
-        return copy
+    class Group:
+        def __init__(self, sems, members):
+            self.sem, self.size = sems.at[len(members)], 0
+            members.append(self)
+
+        def wait(self):
+            span = wg.at[pl.ds(0, self.size // (2 * FF))]
+            pltpu.make_async_copy(span, span, self.sem).wait()
+
+    arrivals, departures = [], []
+
+    def incoming():
+        return Group(recv_sem, arrivals)
+
+    def outgoing():
+        return Group(send_sem, departures)
+
+    def send(src, dst, device, out, into):
+        pltpu.make_async_remote_copy(
+            src, dst, out.sem, into.sem, device_id=device, device_id_type=MESH
+        ).start()
+        size = 2 * math.prod(src.shape)
+        out.size += size
+        into.size += size
 
     ids = [jnp.broadcast_to(ids_ref[k : k + 1, :].astype(F32), (TOK, TOK)) for k in range(2)]
     wts = [jnp.broadcast_to(wts_ref[k : k + 1, :], (TOK, TOK)) for k in range(2)]
@@ -90,21 +103,23 @@
         return sum(dot(pick[q], values[:, q * QUARTER : (q + 1) * QUARTER]) for q in range(4))
 
     def trade(n):
-        copies = [send(box_s.at[n, d[1]], box_r.at[n, rep], d) for d in traders]
+        out, into = outgoing(), incoming()
+        for d in traders:
+            send(box_s.at[n, d[1]], box_r.at[n, rep], d, out, into)
         box_r[n, rep] = box_s[n, rep]
-        return copies
+        return into
 
     get_tok.wait()
     box_s[0] = pack(tok[...]).astype(BF16).reshape(4, 16, QUARTER)
     pl.semaphore_wait(barrier, len(neighbours))
     trade_x = trade(0)
     get_cot.wait()
+    get_w = [fetch(wg_hbm.at[0], wg, 2), fetch(wu_hbm.at[0], wu, 3), fetch(wd_hbm.at[0], wd, 4)]
     box_s[1] = (pack(cot[...]) * row_weight).astype(BF16).reshape(4, 16, QUARTER)
     trade_u = trade(1)
 
-    def settle(copies, n, buf):
-        for copy in copies:
-            copy.wait_recv()
+    def settle(into, n, buf):
+        into.wait()
         r = lax.broadcasted_iota(jnp.int32, (16, 64), 0)
         s = lax.broadcasted_iota(jnp.int32, (16, 64), 1)
         blocks = box_r[n].reshape(64, QUARTER)
@@ -128,79 +143,106 @@
     def gather_y_first(part, buf):
         _, _, (_, a, b) = part
         (up_a, down_a), (up_b, down_b) = sides(a), sides(b)
-
-        def push(where, device, y=(0, 2)):
-            ref = buf.at[at(part, **where, y=y)]
-            return send(ref, ref, device)
-
-        def pass_on(up, down, where):
-            up.wait_recv()
-            up = push({**where, b: (before[b], 1)}, up_b, (0, 1))
-            down.wait_recv()
-            return up, push({**where, b: (after[b], 1)}, down_b, (1, 1))
-
-        ref = buf.at[at(part)]
-        y = send(ref, ref, sides("y")[0])
-        yield
-        y.wait_recv()
-        au, ad = push({}, up_a), push({}, down_a)
-        x0 = push({}, up_b), push({}, down_b)
-        yield
-        low, high, other = {a: (before[a], 1)}, {a: (after[a], 1)}, {a: (far[a], 1)}
-        au.wait_recv()
-        au = push(low, up_a, (0, 1))
-        ad.wait_recv()
-        ad = push(high, down_a, (1, 1))
-        x1 = push(low, up_b), push(low, down_b)
-        x2 = push(high, up_b), push(high, down_b)
-        yield
-        ends = [*pass_on(*x0, {})]
-        yield
-        au.wait_recv()
-        ad.wait_recv()
-        x3 = push(other, up_b), push(other, down_b)
-        yield
-        ends += [*pass_on(*x1, low), *pass_on(*x2, high)]
-        yield
-        ends += [*pass_on(*x3, other)]
-        yield
-        for copy in ends:
-            copy.wait_recv()
+        low, high, other = before[a], after[a], far[a]
+        rows_y = [own["y"], 1 - own["y"]]
+        out = outgoing()
+
+        def push(j, device, into, pa=None, pb=None):
+            where = {"y": (rows_y[j], 1)}
+            if pa is not None:
+                where[a] = (pa, 1)
+            if pb is not None:
+                where[b] = (pb, 1)
+            ref = buf.at[at(part, **where)]
+            send(ref, ref, device, out, into)
+
+        def either(j, first, second):
+            return jnp.where(rows_y[j] == 0, first, second)
+
+        def onward(j, axis, up, down, into, **fixed):
+            device = tuple(either(j, u, d) for u, d in zip(up, down))
+            spot = either(j, before[axis], after[axis])
+            push(j, device, into, **{"pa" if axis == a else "pb": spot}, **fixed)
+
+        def both(j, into, pa=None):
+            push(j, up_b, into, pa)
+            push(j, down_b, into, pa)
+
+        def begin(j):
+            push(j, up_a, first_a[j])
+            push(j, down_a, first_a[j])
+            both(j, first_b[j])
+
+        first_a, first_b, far_a, near, last = ([incoming(), incoming()] for _ in range(5))
+        over, ends = incoming(), incoming()
+        push(0, sides("y")[0], over)
+        begin(0)
+        yield
+        over.wait()
+        begin(1)
+        yield
+        for j in range(2):
+            first_a[j].wait()
+            onward(j, a, up_a, down_a, far_a[j])
+            both(j, near[j], low)
+            both(j, near[j], high)
+            yield
+        for j in range(2):
+            first_b[j].wait()
+            onward(j, b, up_b, down_b, ends)
+        yield
+        for j in range(2):
+            far_a[j].wait()
+            both(j, last[j], other)
+        yield
+        for j in range(2):
+            near[j].wait()
+            for p in (low, high):
+                onward(j, b, up_b, down_b, ends, pa=p)
+        yield
+        for j in range(2):
+            last[j].wait()
+            onward(j, b, up_b, down_b, ends, pa=other)
+        yield
+        ends.wait()
 
     def gather_y_last(part, buf):
         _, _, (a, b, _) = part
         (up_a, down_a), (up_b, down_b) = sides(a), sides(b)
         over = sides("y")[0]
-
-        def push(where, device, cut=None):
+        out = outgoing()
+
+        def push(where, device, into, cut=None):
             ref = buf.at[at(part, cut, **where)]
-            return send(ref, ref, device)
-
-        au, ad = push({}, up_a), push({}, down_a)
-        yield
-        au.wait_recv()
-        au = push({a: (before[a], 1)}, up_a, 0)
-        ad.wait_recv()
-        ad = push({a: (after[a], 1)}, down_a, 1)
-        yield
-        au.wait_recv()
-        ad.wait_recv()
+            send(ref, ref, device, out, into)
+
+        first_a, far_a, first_b, far_b, ends = (incoming() for _ in range(5))
+        push({}, up_a, first_a)
+        push({}, down_a, first_a)
+        yield
+        yield
+        first_a.wait()
+        push({a: (before[a], 1)}, up_a, far_a, 0)
+        push({a: (after[a], 1)}, down_a, far_a, 1)
+        yield
+        far_a.wait()
         whole = {a: all_of(a)}
-        bu, bd = push(whole, up_b), push(whole, down_b)
-        ends = [push(whole, over)]
-        yield
-        bu.wait_recv()
-        bu = push({a: (0, 2), b: (before[b], 1)}, up_b)
-        bd.wait_recv()
-        bd = push({a: (2, 2), b: (after[b], 1)}, down_b)
-        ends += [push({**whole, b: (before[b], 1)}, over), push({**whole, b: (after[b], 1)}, over)]
-        yield
-        bu.wait_recv()
-        bd.wait_recv()
-        ends += [push({**whole, b: (far[b], 1)}, over)]
-        yield
-        for copy in ends:
-            copy.wait_recv()
+        push(whole, up_b, first_b)
+        push(whole, down_b, first_b)
+        push(whole, over, ends)
+        yield
+        yield
+        first_b.wait()
+        push({a: (0, 2), b: (before[b], 1)}, up_b, far_b)
+        push({a: (2, 2), b: (after[b], 1)}, down_b, far_b)
+        push({**whole, b: (before[b], 1)}, over, ends)
+        push({**whole, b: (after[b], 1)}, over, ends)
+        yield
+        far_b.wait()
+        push({**whole, b: (far[b], 1)}, over, ends)
+        yield
+        yield
+        ends.wait()
 
     def gather(part, buf):
         return (gather_y_first if part[2][0] == "y" else gather_y_last)(part, buf)
@@ -214,26 +256,31 @@
     landing = list(landing)
 
     class Ring:
-        def __init__(self, part, buf, axis, split, where):
+        def __init__(self, part, buf, axis, split, where, out):
             self.up, self.down = sides(axis)
-            self.axis, self.buf, self.where = axis, buf, where
+            self.axis, self.buf, self.out = axis, buf, out
             self.via = [landing.pop(0) for _ in range(2)]
             self.land = [landing.pop(0) for _ in range(2)]
             self.half = [(lambda p, i=i: at(part, **{**where, axis: (p, 1)}, **split(i)[0])) for i in range(2)]
             self.part_of = [split(i)[1] for i in range(2)]
+            self.passing, self.landed = incoming(), incoming()
 
         def far(self):
             p = far[self.axis]
-            self.o0 = send(self.buf.at[self.half[0](p)], self.via[0], self.up)
-            self.o1 = send(self.buf.at[self.half[1](p)], self.via[1], self.down)
+            send(self.buf.at[self.half[0](p)], self.via[0], self.up, self.out, self.passing)
+            send(self.buf.at[self.half[1](p)], self.via[1], self.down, self.out, self.passing)
+
+        def to_up(self, i, index):
+            send(self.buf.at[index], self.land[0].at[self.part_of[i]], self.up, self.out, self.landed)
+
+        def to_down(self, i, index):
+            send(self.buf.at[index], self.land[1].at[self.part_of[i]], self.down, self.out, self.landed)
 
         def near_up(self):
-            ref = self.buf.at[self.half[1](after[self.axis])]
-            self.e1 = send(ref, self.land[0].at[self.part_of[1]], self.up)
+            self.to_up(1, self.half[1](after[self.axis]))
 
         def near_down(self):
-            ref = self.buf.at[self.half[0](before[self.axis])]
-            self.e0 = send(ref, self.land[1].at[self.part_of[0]], self.down)
+            self.to_down(0, self.half[0](before[self.axis]))
 
         def start(self):
             self.far()
@@ -241,18 +288,16 @@
             self.near_down()
 
         def middle(self):
-            self.o0.wait_recv()
+            self.passing.wait()
             index = self.half[0](after[self.axis])
             add(self.buf, index, self.via[0])
-            self.f0 = send(self.buf.at[index], self.land[0].at[self.part_of[0]], self.up)
-            self.o1.wait_recv()
+            self.to_up(0, index)
             index = self.half[1](before[self.axis])
             add(self.buf, index, self.via[1])
-            self.f1 = send(self.buf.at[index], self.land[1].at[self.part_of[1]], self.down)
+            self.to_down(1, index)
 
         def end(self, index):
-            for copy in (self.e1, self.e0, self.f0, self.f1):
-                copy.wait_recv()
+            self.landed.wait()
             add(self.buf, index, *self.land)
 
     def by_y(i):
@@ -271,39 +316,38 @@
     def scatter_y_last(part, buf):
         _, _, (_, a, b) = part
         spots = {"far": (far[a], 1), "low": (before[a], 1), "high": (after[a], 1), "own": (own[a], 1)}
-        rings = {k: Ring(part, buf, b, by_y, {a: spots[k]}) for k in ("far", "low", "high", "own")}
-        last = Ring(part, buf, a, by_y, {})
-        land_y = landing.pop(0)
+        out = outgoing()
+        rings = {k: Ring(part, buf, b, by_y, {a: spots[k]}, out) for k in ("far", "low", "high", "own")}
+        last = Ring(part, buf, a, by_y, {}, out)
+        land_y, over = landing.pop(0), incoming()
 
         def finish(k):
             rings[k].end(at(part, **{a: spots[k]}, y=(0, 2)))
 
         def walk():
-            rings["far"].start()
-            rings["low"].start()
-            yield
-            rings["far"].middle()
-            rings["high"].start()
-            yield
-            rings["low"].middle()
+            for ring in rings.values():
+                ring.far()
+            yield
+            for ring in rings.values():
+                ring.middle()
+                ring.near_down()
+                ring.near_up()
+                yield
             finish("far")
             last.far()
-            rings["own"].start()
-            yield
-            rings["high"].middle()
+            yield
             finish("low")
             last.near_down()
-            yield
-            rings["own"].middle()
             finish("high")
             last.near_up()
+            yield
             last.middle()
-            yield
             finish("own")
+            yield
             last.end(at(part, y=(0, 2)))
-            y = send(buf.at[at(part, y=(after["y"], 1))], land_y, sides("y")[0])
-            yield
-            y.wait_recv()
+            send(buf.at[at(part, y=(after["y"], 1))], land_y, sides("y")[0], out, over)
+            yield
+            over.wait()
             add(buf, at(part), land_y)
 
         return walk()
@@ -313,26 +357,30 @@
         whole = {a: all_of(a)}
         spots = [{**whole, b: (p[b], 1)} for p in (far, before, after, own)]
         land_y = [landing.pop(0) for _ in spots]
-        ring = Ring(part, buf, b, by_place(a), {})
-        last = Ring(part, buf, a, by_columns, {})
+        out, over = outgoing(), [incoming() for _ in spots]
+        ring = Ring(part, buf, b, by_place(a), {}, out)
+        last = Ring(part, buf, a, by_columns, {}, out)
 
         def walk():
-            copies = [
-                send(buf.at[at(part, **spot, y=(after["y"], 1))], land, sides("y")[0])
-                for spot, land in zip(spots, land_y)
-            ]
+            def give(*which):
+                for i in which:
+                    src = buf.at[at(part, **spots[i], y=(after["y"], 1))]
+                    send(src, land_y[i], sides("y")[0], out, over[i])
 
             def take(i):
-                copies[i].wait_recv()
+                over[i].wait()
                 add(buf, at(part, **spots[i]), land_y[i])
 
-            yield
+            give(0, 1)
+            yield
+            give(2, 3)
             take(0)
             ring.far()
             yield
             take(1)
+            ring.near_down()
+            yield
             take(2)
-            ring.near_down()
             ring.near_up()
             yield
             take(3)
@@ -429,29 +477,33 @@
     uw = [gather(part, us) for part in PARTS]
     go(uw)
     go(xw)
-    go(xw)
-    go(uw)
-    go(xw)
-    go(xw)
-    go(uw)
-    go(xw)
+    go(uw)
+    go(xw)
+    go(xw)
+    go(xw)
+    go(uw)
+    go(xw)
+    go(uw)
     go(uw)
     go(xw)
     go(uw)
     go(xw)
     for copy in get_w:
         copy.wait()
+    go(xw)
     forward(0)
     go(uw)
     forward(1)
-    go(uw)
     pw = [scatter(part, ps) for part in PARTS]
     qw = [scatter(part, qs) for part in PARTS]
     go(pw)
     go(uw)
     go(pw)
+    go(pw)
+    go(uw)
     backward(0)
     go(pw)
+    go(pw)
     backward(1)
     go(pw)
     row_grads(0)
@@ -460,6 +512,10 @@
     go(qw)
     go(pw)
     go(qw)
+    go(qw)
+    go(pw)
+    go(qw)
+    go(qw)
     grad_in(0)
     go(pw)
     trade_m = send_back(2, ps)
@@ -468,21 +524,20 @@
     go(qw)
     grad_out()
     go(qw)
-    for copy in trade_m:
-        copy.wait_recv()
+    trade_m.wait()
     for q in range(4):
         cols = slice(q * QUARTER, (q + 1) * QUARTER)
         out_m[:, cols] = (weight[0] * spread(two[0], q, 2) + weight[1] * spread(two[1], q, 2)).astype(BF16)
     go(qw)
     go(qw)
     trade_g = send_back(3, qs)
-    for copy in trade_g:
-        copy.wait_recv()
+    trade_g.wait()
     for q in range(4):
         cols = slice(q * QUARTER, (q + 1) * QUARTER)
         out_g[:, cols] = spread(two[0] + two[1], q, 3).astype(BF16)
-    for copy in sent:
-        copy.wait_send()
+    for group in departures:
+        group.wait()
+    assert len(arrivals) == ARRIVALS and len(departures) == DEPARTURES
 
 
 def landings(part):
@@ -520,8 +575,8 @@
         vm(512, FF, dtype=F32), vm(512, FF, dtype=F32), vm(512, FF), vm(512, 2 * FF),
         vm(4, 4, 16, QUARTER), vm(4, 4, 16, QUARTER),
         pltpu.SemaphoreType.DMA((5,)),
-        pltpu.SemaphoreType.DMA((COPIES,)),
-        pltpu.SemaphoreType.DMA((COPIES,)),
+        pltpu.SemaphoreType.DMA((DEPARTURES,)),
+        pltpu.SemaphoreType.DMA((ARRIVALS,)),
     ]
     scratch += [vm(*s) for _ in range(2) for part in PARTS for s in landings(part)]
     any_spec = pl.BlockSpec(memory_space=pl.ANY)

time: 125 us -> 120 us (0.960)
  Pallas kernels: 124 us -> 119 us
    pallas_call x1, Pallas kernels: 120 us -> 116 us  [local(): pl.pallas_call(kernel, out_shape=(vm(TOK, D), vm(TOK, D), vm(D, FF), vm(D...]
where the time goes in v3:
time: 120 us
  Pallas kernels  119 us (99%)
    pallas_call x1, Pallas kernels, local(): pl.pallas_call(kernel, out_shape=(vm(TOK, D), vm(TOK, D), vm(D, FF), vm(D...  116 us
    pallas_call x1, Pallas kernels, local(): pl.pallas_call(write_out, out_shape=(shape((TOK, D), BF16), shape((TOK, D...  3.38 us

profile of v3, /device:TPU:1, one launch (start us, length us, event | category | flops | bytes accessed | tf_op | source)
XLA Modules:
  0.0 120.1 jit_solution(9252338102901025900)
XLA Ops:
  0.6 116.1 %moe.1 = (bf16[128,4096]{1,0:T(8,128)(2,1)S(1)}, bf16[128,4096]{1,0:T(8,128)(2,1)S(1)}, bf16[4096,256]{1,0:T(8,128)(2,1)S(1)}, bf16[4096,256]{1,0:T(8,128)(2,1)S(1)}, bf16[256,4096]{1,0:T(8,128)(2,1)S(1)}) custom-call(s32[2,128]{1,0:T(2,128)} %bitcast.2, f32[2,128]{1,0:T(2,128)} %bitcast.3, bf16[128,4096]{1,0:T(8,128)(2,1)} %tok_hbm.1, ...), custom_call_target="tpu_custom_call" | custom-call | flops 9663676416 | bytes 16777216 | tf_op jit(solution)/shard_map/moe/pallas_call | solution.py:585
  116.7 3.4 %write_out.1 = (bf16[128,4096]{1,0:T(8,128)(2,1)}, bf16[128,4096]{1,0:T(8,128)(2,1)}, bf16[1,4096,256]{2,1,0:T(8,128)(2,1)}, bf16[1,4096,256]{2,1,0:T(8,128)(2,1)}, bf16[1,256,4096]{2,1,0:T(8,128)(2,1)}) custom-call(bf16[128,4096]{1,0:T(8,128)(2,1)S(1)} %get-tuple-element.10.refs_0_, bf16[128,4096]{1,0:T(8,128)(2,1)S(1)} %get-tuple-element.11.refs_1_, ...), custom_call_target="tpu_custom_call" | custom-call | tf_op jit(solution)/shard_map/write_out/pallas_call | solution.py:601

commit v4 on v3

--- a/solution.py
+++ b/solution.py
@@ -374,6 +374,7 @@
             give(0, 1)
             yield
             give(2, 3)
+            yield
             take(0)
             ring.far()
             yield
@@ -405,47 +406,54 @@
     def rows(i):
         return pl.ds(i * 256, 256)
 
-    def forward(i):
-        z = pl.ds(i * 2, 2)
-        x = xs[z].reshape(256, D)
+    def hidden(i):
+        x = xs[pl.ds(i * 2, 2)].reshape(256, D)
         g = dot(x, wg[...])
         u = dot(x, wu[...])
         s = 1.0 / (1.0 + jnp.exp(-g))
         a = g * s
-        h = (a * u).astype(BF16)
         act[rows(i), :] = a
         fac[rows(i), :] = u * s * (1.0 + g * (1.0 - s))
-        hid[rows(i), :] = h
-
-        @pl.loop(0, 8)
+        hid[rows(i), :] = (a * u).astype(BF16)
+
+    def by_block(p, body):
+        lo, hi, _ = PARTS[p]
+
+        @pl.loop(lo // 512, hi // 512)
         def _(n):
             cols = pl.ds(pl.multiple_of(n * 512, 512), 512)
-            ps[z, :, :, :, cols] = dot(h, wd[:, cols]).astype(BF16).reshape(2, 2, 4, SLOT, 512)
+            for i in range(2):
+                body(i, cols)
+
+    def routed(p):
+        def body(i, cols):
+            r = dot(hid[rows(i), :], wd[:, cols])
+            ps[pl.ds(i * 2, 2), :, :, :, cols] = r.astype(BF16).reshape(2, 2, 4, SLOT, 512)
+
+        by_block(p, body)
 
     def backward(i):
         d = dot(us[pl.ds(i * 2, 2)].reshape(256, D), wd[...], 1, 1)
         dgu[rows(i), 0:FF] = (d * fac[rows(i), :]).astype(BF16)
         dgu[rows(i), FF : 2 * FF] = (d * act[rows(i), :]).astype(BF16)
 
-    def row_grads(i):
-        dg, du = dgu[rows(i), 0:FF], dgu[rows(i), FF : 2 * FF]
-
-        @pl.loop(0, 8)
-        def _(n):
-            cols = pl.ds(pl.multiple_of(n * 512, 512), 512)
-            g = dot(dg, wg[cols, :], 1, 1) + dot(du, wu[cols, :], 1, 1)
+    def row_grads(p):
+        def body(i, cols):
+            g = dot(dgu[rows(i), 0:FF], wg[cols, :], 1, 1) + dot(dgu[rows(i), FF : 2 * FF], wu[cols, :], 1, 1)
             qs[pl.ds(i * 2, 2), :, :, :, cols] = g.astype(BF16).reshape(2, 2, 4, SLOT, 512)
 
+        by_block(p, body)
+
     def grad_in(i):
-        @pl.loop(4 * i, 4 * i + 4)
+        @pl.loop(2 * i, 2 * i + 2)
         def _(n):
             cols = pl.ds(pl.multiple_of(n * 512, 512), 512)
             g = dot(xs[:, :, :, :, cols].reshape(512, 512), dgu[...], 0, 0)
             gg[cols, :] = g[:, 0:FF].astype(BF16)
             gu[cols, :] = g[:, FF : 2 * FF].astype(BF16)
 
-    def grad_out():
-        @pl.loop(0, 8)
+    def grad_out(i):
+        @pl.loop(4 * i, 4 * i + 4)
         def _(n):
             cols = pl.ds(pl.multiple_of(n * 512, 512), 512)
             gd[:, cols] = dot(hid[...], us[:, :, :, :, cols].reshape(512, 512), 0, 0).astype(BF16)
@@ -472,65 +480,184 @@
 
     settle(trade_x, 0, xs)
     xw = [gather(part, xs) for part in PARTS]
-    go(xw)
+    go(xw, (0,))
+    go(xw, (1,))
+    go(xw, (2,))
+    go(xw, (3,))
     settle(trade_u, 1, us)
     uw = [gather(part, us) for part in PARTS]
-    go(uw)
-    go(xw)
-    go(uw)
-    go(xw)
-    go(xw)
-    go(xw)
-    go(uw)
-    go(xw)
-    go(uw)
-    go(uw)
-    go(xw)
-    go(uw)
-    go(xw)
+    go(xw, (3,))
+    go(xw, (2,))
+    go(uw, (0,))
+    go(uw, (3,))
+    go(uw, (3,))
+    go(uw, (2,))
+    go(xw, (0,))
+    go(xw, (0,))
+    go(uw, (2,))
+    go(uw, (1,))
+    go(xw, (1,))
+    go(xw, (3,))
+    go(xw, (2,))
+    go(xw, (1,))
+    go(uw, (0,))
+    go(uw, (0,))
+    go(uw, (3,))
+    go(uw, (2,))
+    go(uw, (1,))
+    go(xw, (0,))
+    go(xw, (0,))
+    go(uw, (1,))
+    go(xw, (2,))
+    go(xw, (2,))
+    go(xw, (1,))
+    go(xw, (3,))
+    go(xw, (3,))
+    go(xw, (1,))
+    go(uw, (0,))
+    go(uw, (0,))
+    go(xw, (0,))
+    go(uw, (2,))
+    go(uw, (2,))
+    go(uw, (3,))
+    go(uw, (3,))
+    go(uw, (1,))
+    go(uw, (1,))
+    go(xw, (0,))
+    go(xw, (3,))
+    go(xw, (1,))
+    go(xw, (1,))
+    go(xw, (2,))
+    go(uw, (0,))
+    go(uw, (3,))
+    go(uw, (0,))
+    go(xw, (0,))
+    go(xw, (3,))
+    go(xw, (3,))
+    go(uw, (2,))
+    go(uw, (1,))
+    go(xw, (1,))
+    go(uw, (1,))
+    go(xw, (2,))
+    go(xw, (2,))
+    go(uw, (3,))
+    go(uw, (3,))
+    go(xw, (3,))
+    go(uw, (0,))
+    go(uw, (1,))
+    go(xw, (1,))
+    go(xw, (0,))
+    go(xw, (2,))
     for copy in get_w:
         copy.wait()
-    go(xw)
-    forward(0)
-    go(uw)
-    forward(1)
+    hidden(0)
+    hidden(1)
+    go(uw, (0,))
+    go(uw, (3,))
+    go(uw, (2,))
+    go(uw, (2,))
+    go(uw, (1,))
+    routed(1)
     pw = [scatter(part, ps) for part in PARTS]
     qw = [scatter(part, qs) for part in PARTS]
-    go(pw)
-    go(uw)
-    go(pw)
-    go(pw)
-    go(uw)
+    go(pw, (1,))
+    routed(0)
+    go(pw, (0,))
+    go(uw, (2,))
+    backward(1)
+    routed(2)
+    go(pw, (1,))
+    go(pw, (2,))
+    go(pw, (2,))
     backward(0)
-    go(pw)
-    go(pw)
-    backward(1)
-    go(pw)
+    go(pw, (1,))
+    go(pw, (0,))
+    row_grads(3)
+    go(qw, (3,))
+    go(qw, (3,))
+    go(pw, (1,))
+    go(pw, (0,))
+    go(pw, (1,))
+    go(pw, (2,))
+    go(pw, (0,))
+    row_grads(1)
+    go(qw, (1,))
+    go(pw, (1,))
+    go(pw, (2,))
+    go(pw, (2,))
+    go(pw, (0,))
+    go(pw, (0,))
+    row_grads(2)
+    go(qw, (2,))
+    go(qw, (2,))
     row_grads(0)
-    go(pw)
-    row_grads(1)
-    go(qw)
-    go(pw)
-    go(qw)
-    go(qw)
-    go(pw)
-    go(qw)
-    go(qw)
+    go(qw, (0,))
+    go(qw, (3,))
+    go(qw, (3,))
+    go(pw, (1,))
+    go(pw, (2,))
+    go(pw, (0,))
+    go(qw, (3,))
+    go(qw, (1,))
+    go(pw, (1,))
+    routed(3)
+    go(qw, (1,))
+    go(pw, (3,))
+    go(pw, (3,))
+    grad_in(2)
+    go(qw, (2,))
+    go(qw, (1,))
+    go(qw, (1,))
+    go(qw, (2,))
+    go(qw, (0,))
+    go(pw, (0,))
+    grad_out(0)
+    go(qw, (0,))
+    go(qw, (0,))
+    go(qw, (3,))
+    go(qw, (2,))
+    grad_in(3)
+    go(qw, (0,))
+    go(pw, (3,))
+    grad_out(1)
+    go(qw, (1,))
+    go(pw, (3,))
+    go(pw, (1,))
+    go(pw, (2,))
+    go(qw, (2,))
+    go(pw, (3,))
     grad_in(0)
-    go(pw)
+    grad_in(1)
+    go(qw, (0,))
+    go(qw, (1,))
+    go(pw, (1,))
+    go(pw, (0,))
+    go(qw, (3,))
+    go(qw, (0,))
+    go(pw, (3,))
+    go(pw, (2,))
+    go(pw, (0,))
+    go(qw, (0,))
+    go(qw, (1,))
+    go(qw, (2,))
+    go(pw, (3,))
+    go(pw, (2,))
+    go(qw, (3,))
+    go(qw, (0,))
+    go(qw, (2,))
+    go(qw, (1,))
+    go(pw, (3,))
+    go(qw, (3,))
+    go(qw, (2,))
+    go(qw, (0,))
+    go(pw, (3,))
     trade_m = send_back(2, ps)
-    go(qw)
-    grad_in(1)
-    go(qw)
-    grad_out()
-    go(qw)
+    go(qw, (1,))
+    trade_g = send_back(3, qs)
     trade_m.wait()
     for q in range(4):
         cols = slice(q * QUARTER, (q + 1) * QUARTER)
         out_m[:, cols] = (weight[0] * spread(two[0], q, 2) + weight[1] * spread(two[1], q, 2)).astype(BF16)
-    go(qw)
-    go(qw)
-    trade_g = send_back(3, qs)
     trade_g.wait()
     for q in range(4):
         cols = slice(q * QUARTER, (q + 1) * QUARTER)

time: 120 us -> 110 us (0.917)
  Pallas kernels: 119 us -> 109 us
    pallas_call x1, Pallas kernels: 116 us -> 106 us  [local(): pl.pallas_call(kernel, out_shape=(vm(TOK, D), vm(TOK, D), vm(D, FF), vm(D...]
where the time goes in v4:
time: 110 us
  Pallas kernels  109 us (99%)
    pallas_call x1, Pallas kernels, local(): pl.pallas_call(kernel, out_shape=(vm(TOK, D), vm(TOK, D), vm(D, FF), vm(D...  106 us
    pallas_call x1, Pallas kernels, local(): pl.pallas_call(write_out, out_shape=(shape((TOK, D), BF16), shape((TOK, D...  3.38 us

profile of v4, /device:TPU:1, one launch (start us, length us, event | category | flops | bytes accessed | tf_op | source)
XLA Modules:
  0.0 110.1 jit_solution(9494516367735838442)
XLA Ops:
  0.6 105.9 %moe.1 = (bf16[128,4096]{1,0:T(8,128)(2,1)S(1)}, bf16[128,4096]{1,0:T(8,128)(2,1)S(1)}, bf16[4096,256]{1,0:T(8,128)(2,1)S(1)}, bf16[4096,256]{1,0:T(8,128)(2,1)S(1)}, bf16[256,4096]{1,0:T(8,128)(2,1)S(1)}) custom-call(s32[2,128]{1,0:T(2,128)} %bitcast.2, f32[2,128]{1,0:T(2,128)} %bitcast.3, bf16[128,4096]{1,0:T(8,128)(2,1)} %tok_hbm.1, ...), custom_call_target="tpu_custom_call" | custom-call | flops 9663676416 | bytes 16777216 | tf_op jit(solution)/shard_map/moe/pallas_call | solution.py:712
  106.6 3.4 %write_out.1 = (bf16[128,4096]{1,0:T(8,128)(2,1)}, bf16[128,4096]{1,0:T(8,128)(2,1)}, bf16[1,4096,256]{2,1,0:T(8,128)(2,1)}, bf16[1,4096,256]{2,1,0:T(8,128)(2,1)}, bf16[1,256,4096]{2,1,0:T(8,128)(2,1)}) custom-call(bf16[128,4096]{1,0:T(8,128)(2,1)S(1)} %get-tuple-element.10.refs_0_, bf16[128,4096]{1,0:T(8,128)(2,1)S(1)} %get-tuple-element.11.refs_1_, ...), custom_call_target="tpu_custom_call" | custom-call | tf_op jit(solution)/shard_map/write_out/pallas_call | solution.py:728
